TPU v7x, 256 devices: a whole 4x4x8 slice. The times are simulated.
256 devices in a mesh: band: 64 (over z, y, core), chan: 4 (over x).
Axes of the slice: x: 4, y: 4, z: 8, core: 2. Of those that a mesh axis runs over, the one named last changes fastest.
Arguments:
- grid_in: bfloat16 [524288, 474], P('band'), may hold values from -6 to 6
- w_embed: bfloat16 [474, 512], P(None, 'chan'), may hold values from -0.25 to 0.25
- send_order: int32 [64, 64], P('band'), may hold values from 0 to 63, each once within a row
- enc_coef: bfloat16 [6144, 128, 128], P('band'), may hold values from -0.125 to 0.125
- enc_slot: int32 [64, 96], P('band'), may hold values from 0 to 63
- enc_dest: int32 [64, 96], P('band'), may hold values from 0 to 4
- mesh_in: bfloat16 [40960, 512], P('band', 'chan'), may hold values from -6 to 6
- proc_coef: bfloat16 [3072, 128, 128], P('band'), may hold values from -0.15625 to 0.15625
- proc_src: int32 [64, 48], P('band'), may hold values from 0 to 14
- proc_dest: int32 [64, 48], P('band'), may hold values from 0 to 4
- w_node: bfloat16 [512, 512], P(None, 'chan'), may hold values from -0.25 to 0.25
- out_grad: bfloat16 [40960, 512], P('band', 'chan'), may hold values from -6 to 6
Outputs:
- mesh_out: bfloat16 [40960, 512], P('band', 'chan')
- mesh_grad: float32 [40960, 512], P('band', 'chan')
- grad_embed: float32 [474, 512], P(None, 'chan')
- grad_node: float32 [512, 512], P(None, 'chan')
All inputs are finite; a program needn't handle non-finite values.
Results may differ from a plain program's by a relative error of at most 0.006.
Values may be sent and summed in bfloat16 or wider, within the bound.
A program may use at most 128 MiB of HBM per device.

v0:
```python
import jax
import jax.numpy as jnp
from jax import lax
from jax.sharding import PartitionSpec as P


def with_halo(block, sides, width):
    for axis, dim in sides:
        count = lax.axis_size(axis)
        forward = [(i, i + 1) for i in range(count - 1)]
        backward = [(target, source) for source, target in forward]
        low = lax.ppermute(
            lax.slice_in_dim(block, block.shape[dim] - width, None, axis=dim), axis, forward
        )
        high = lax.ppermute(lax.slice_in_dim(block, 0, width, axis=dim), axis, backward)
        block = jnp.concatenate([low, block, high], axis=dim)
    return block


def from_behind(value, axis, steps):
    count = lax.axis_size(axis)
    first, last = (max(0, -steps), min(count, count - steps))
    return lax.ppermute(value, axis, [(source, source + steps) for source in range(first, last)])


def silu_slope(values):
    sigma = jax.nn.sigmoid(values)
    return sigma * (1.0 + values * (1.0 - sigma))


def select_matrix(targets, count):
    return (targets[None, :] == jnp.arange(count, dtype=jnp.int32)[:, None]).astype(jnp.float32)


def collect(weights, source, source_ids, dest_ids, count):
    picked = source[source_ids]
    messages = jnp.einsum("pij,pjc->pic", weights, picked, preferred_element_type=jnp.float32)
    return jnp.einsum(
        "bp,pic->bic", select_matrix(dest_ids, count), messages, precision=lax.Precision.HIGHEST
    )


def spread(weights, target, source_ids, dest_ids, count):
    picked = target[dest_ids]
    messages = jnp.einsum("pji,pjc->pic", weights, picked, preferred_element_type=jnp.float32)
    return jnp.einsum(
        "sp,pic->sic", select_matrix(source_ids, count), messages, precision=lax.Precision.HIGHEST
    )


def on_device(
    grid_in,
    w_embed,
    send_order,
    enc_coef,
    enc_slot,
    enc_dest,
    mesh_in,
    proc_coef,
    proc_src,
    proc_dest,
    w_node,
    out_grad,
):
    block_size = enc_coef.shape[1]
    width_here = w_embed.shape[1]
    send_list = send_order[0]
    grid_blocks = send_list.shape[0]
    mesh_blocks = mesh_in.shape[0] // block_size
    pre_grid = jnp.dot(grid_in, w_embed, preferred_element_type=jnp.float32)
    latent = jax.nn.silu(pre_grid).astype(jnp.bfloat16).reshape(grid_blocks, block_size, width_here)
    received = lax.all_to_all(latent[send_list], "band", split_axis=0, concat_axis=0, tiled=True)
    enc_pre = collect(enc_coef, received, enc_slot[0], enc_dest[0], mesh_blocks).reshape(
        -1, width_here
    )
    mesh_one = (mesh_in.astype(jnp.float32) + jax.nn.silu(enc_pre)).astype(jnp.bfloat16)
    extended = with_halo(
        mesh_one.reshape(mesh_blocks, block_size, width_here), (("band", 0),), mesh_blocks
    )
    proc_pre = collect(proc_coef, extended, proc_src[0], proc_dest[0], mesh_blocks).reshape(
        -1, width_here
    )
    hidden = jax.nn.silu(proc_pre).astype(jnp.bfloat16)
    shard_part = lax.all_gather(hidden, "chan", axis=1, tiled=True)
    mixed = jnp.dot(shard_part, w_node, preferred_element_type=jnp.float32)
    grad_rows = jnp.einsum("mk,mc->kc", shard_part, out_grad, preferred_element_type=jnp.float32)
    mesh_out = (mesh_one.astype(jnp.float32) + mixed).astype(jnp.bfloat16)
    partial_hidden = jnp.einsum("mc,kc->mk", out_grad, w_node, preferred_element_type=jnp.float32)
    grad_hidden = lax.psum_scatter(partial_hidden, "chan", scatter_dimension=1, tiled=True)
    grad_proc = (
        (grad_hidden * silu_slope(proc_pre))
        .astype(jnp.bfloat16)
        .reshape(mesh_blocks, block_size, width_here)
    )
    grad_extended = spread(proc_coef, grad_proc, proc_src[0], proc_dest[0], 3 * mesh_blocks)
    from_upper = from_behind(grad_extended[:mesh_blocks], "band", -1)
    from_lower = from_behind(grad_extended[2 * mesh_blocks :], "band", 1)
    mesh_sum = grad_extended[mesh_blocks : 2 * mesh_blocks] + from_upper + from_lower
    mesh_grad = out_grad.astype(jnp.float32) + mesh_sum.reshape(-1, width_here)
    grad_enc = (
        (mesh_grad * silu_slope(enc_pre))
        .astype(jnp.bfloat16)
        .reshape(mesh_blocks, block_size, width_here)
    )
    grad_received = spread(enc_coef, grad_enc, enc_slot[0], enc_dest[0], received.shape[0])
    grad_sent = lax.all_to_all(grad_received, "band", split_axis=0, concat_axis=0, tiled=True)
    grad_grid = jnp.zeros_like(grad_sent).at[send_list].set(grad_sent).reshape(-1, width_here)
    grad_pre = (grad_grid * silu_slope(pre_grid)).astype(jnp.bfloat16)
    grad_embed_part = jnp.einsum("gc,gl->cl", grid_in, grad_pre, preferred_element_type=jnp.float32)
    grad_embed, grad_node = lax.psum((grad_embed_part, grad_rows), "band")
    return (mesh_out, mesh_grad, grad_embed, grad_node)


def solution(mesh):
    return jax.shard_map(
        on_device,
        mesh=mesh,
        in_specs=(
            P("band", None),
            P(None, "chan"),
            P("band", None),
            P("band", None, None),
            P("band", None),
            P("band", None),
            P("band", "chan"),
            P("band", None, None),
            P("band", None),
            P("band", None),
            P(None, "chan"),
            P("band", "chan"),
        ),
        out_specs=(P("band", "chan"), P("band", "chan"), P(None, "chan"), P(None, "chan")),
        check_vma=False,
    )
```

profile of v0, /device:TPU:1, one launch (start us, length us, event | category | flops | bytes accessed | tf_op | source)
XLA Modules:
  0.0 509.7 jit_solution(3028754570363195178)
XLA Ops:
  8.0 8.5 %multiply_convert_fusion = (bf16[8192,128]{1,0:T(8,128)(2,1)}, f32[8192,128]{1,0:T(8,128)}) fusion(bf16[8192,474]{0,1:T(8,128)(2,1)} %param.12, bf16[474,128]{1,0:T(8,128)(2,1)} %param.13), kind=kOutput, calls=%fused_computation.8 | convolution fusion | flops 999292928 | bytes 14178816 | tf_op jit(solution)/shard_map/dot_general | solution.py:70
  16.5 3.7 gather_fusion
  20.2 13.5 %all-to-all-start = ((bf16[64,128,128]{2,1,0:T(8,128)(2,1)}), bf16[64,128,128]{2,1,0:T(8,128)(2,1)}, u32[]{:S(2)}, u32[]{:S(2)}) async-start(bf16[64,128,128]{2,1,0:T(8,128)(2,1)} %gather_fusion), calls=%async_computation | async-start | bytes 4194304 | tf_op jit(solution)/shard_map/all_to_all | solution.py:72
  35.3 48.0 %all-to-all-done = bf16[64,128,128]{2,1,0:T(8,128)(2,1)} async-done(((bf16[64,128,128]{2,1,0:T(8,128)(2,1)}), bf16[64,128,128]{2,1,0:T(8,128)(2,1)}, u32[]{:S(2)}, u32[]{:S(2)}) %all-to-all-start) | async-done | bytes 2097184 | tf_op jit(solution)/shard_map/all_to_all | solution.py:72
  83.3 4.4 gather_fusion.1
  87.7 6.9 %convolution_bitcast_fusion.1 = f32[96,128,128]{1,2,0:T(8,128)} fusion(bf16[96,128,128]{2,1,0:T(8,128)(2,1)} %gather_fusion.1, bf16[96,128,128]{2,1,0:T(8,128)(2,1)S(1)} %copy-done), kind=kOutput, calls=%fused_computation.11 | convolution fusion | flops 402653184 | bytes 12582912 | tf_op jit(solution)/shard_map/pij,pjc->pic/dot_general | solution.py:37
  94.6 6.7 %copy.30 = f32[96,128,128]{2,0,1:T(8,128)} copy(f32[96,128,128]{1,2,0:T(8,128)} %convolution_bitcast_fusion.1) | data formatting | bytes 12582912 | tf_op jit(solution)/shard_map/pij,pjc->pic/dot_general | solution.py:37
  101.3 4.2 fusion.29
  106.5 5.1 %collective-permute-start = (bf16[5,128,128]{2,1,0:T(8,128)(2,1)S(1)}, bf16[5,128,128]{2,1,0:T(8,128)(2,1)S(1)}, u32[]{:S(2)}, u32[]{:S(2)}) collective-permute-start(bf16[5,128,128]{2,1,0:T(8,128)(2,1)S(1)} %bitcast.132), channel_id=1, source_target_pairs={{0,4},{4,8},{8,12},{12,16},{16,20},{20,24},{24,28},{28,32},{32,36}... | collective-permute-start | bytes 491528 | tf_op jit(solution)/shard_map/ppermute | solution.py:12
  113.8 4.4 collective-permute-done.1
  119.1 3.0 gather_fusion.2
  122.1 4.8 convolution_bitcast_fusion.3
  126.9 3.6 copy.33
  130.4 3.0 fusion.32
  138.1 4.2 convolution_bitcast_fusion.2
  142.3 3.6 copy.36
  145.9 3.0 fusion.25
  151.0 3.9 collective-permute-start.3
  154.9 4.7 collective-permute-done.2
  161.8 2.8 gather_fusion.4
  164.6 5.7 %convolution_bitcast_fusion = f32[96,128,128]{1,2,0:T(8,128)} fusion(bf16[96,128,128]{2,1,0:T(8,128)(2,1)} %gather_fusion.4, bf16[96,128,128]{2,1,0:T(8,128)(2,1)S(1)} %copy-done), kind=kOutput, calls=%fused_computation.10 | convolution fusion | flops 402653184 | bytes 12582912 | tf_op jit(solution)/shard_map/pji,pjc->pic/dot_general | solution.py:45
  170.3 6.7 %copy.39 = f32[96,128,128]{2,0,1:T(8,128)} copy(f32[96,128,128]{1,2,0:T(8,128)} %convolution_bitcast_fusion) | data formatting | bytes 12582912 | tf_op jit(solution)/shard_map/pji,pjc->pic/dot_general | solution.py:45
  177.0 4.8 fusion.21
  181.9 4.5 copy.40
  186.4 15.1 %all-to-all-start.1 = ((f32[64,128,128]{2,1,0:T(8,128)}), f32[64,128,128]{2,1,0:T(8,128)}, u32[]{:S(2)}, u32[]{:S(2)}) async-start(f32[64,128,128]{2,1,0:T(8,128)} %copy.40), calls=%async_computation.2 | async-start | bytes 8388608 | tf_op jit(solution)/shard_map/all_to_all | solution.py:106
  201.6 14.6 %all_gather.3 = bf16[640,512]{1,0:T(8,128)(2,1)S(1)} all-gather(bf16[640,128]{1,0:T(8,128)(2,1)S(1)} %copy-done.8), channel_id=1, replica_groups=mesh['band'=64,'chan'=4] {'chan'}, dimensions={1}, use_global_device_ids=true | all-gather | bytes 819200 | tf_op jit(solution)/shard_map/all_gather | solution.py:84
  217.3 78.6 %all-to-all-done.1 = f32[64,128,128]{2,1,0:T(8,128)} async-done(((f32[64,128,128]{2,1,0:T(8,128)}), f32[64,128,128]{2,1,0:T(8,128)}, u32[]{:S(2)}, u32[]{:S(2)}) %all-to-all-start.1) | async-done | bytes 4194336 | tf_op jit(solution)/shard_map/all_to_all | solution.py:106
  295.9 2.5 broadcast_in_dim.2
  298.5 12.1 %scatter_fusion = f32[64,128,128]{2,1,0:T(8,128)} fusion(f32[64,128,128]{2,1,0:T(8,128)} %broadcast_in_dim.2, s32[64]{0:T(128)S(1)} %fusion.36, f32[64,128,128]{2,1,0:T(8,128)} %all-to-all-done.1), kind=kCustom, calls=%fused_computation.5 | custom fusion | bytes 12583168 | tf_op jit(solution)/shard_map/scatter | solution.py:107
  310.5 5.0 fusion
  315.6 6.3 %convolution_bitcast_fusion.4 = f32[474,128]{1,0:T(8,128)} fusion(bf16[8192,128]{1,0:T(8,128)(2,1)S(1)} %fusion, bf16[8192,474]{0,1:T(8,128)(2,1)} %param.12), kind=kOutput, calls=%fused_computation.16 | convolution fusion | flops 994050048 | bytes 10105856 | tf_op jit(solution)/shard_map/gc,gl->cl/dot_general | solution.py:109
  324.0 175.5 %all-reduce.3.cloned.1.call-done = (f32[474,128]{1,0:T(8,128)}, f32[512,128]{1,0:T(8,128)}) async-done(((f32[474,128]{1,0:T(8,128)}, f32[512,128]{1,0:T(8,128)}), (f32[474,128]{1,0:T(8,128)}, f32[512,128]{1,0:T(8,128)})) %all-reduce.3.cloned.1.call-update) | async-done | bytes 504848 | tf_op jit(solution)/shard_map/psum | solution.py:110
  (66 shorter events, 21.8 us)
Async XLA Ops:
  7.2 80.5 %copy-start = (bf16[96,128,128]{2,1,0:T(8,128)(2,1)S(1)}, bf16[96,128,128]{2,1,0:T(8,128)(2,1)}, u32[]{:S(2)}) copy-start(bf16[96,128,128]{2,1,0:T(8,128)(2,1)} %param.15) | copy-start | bytes 9437188
  20.2 13.6 %copy-start.5 = (bf16[640,128]{1,0:T(8,128)(2,1)S(1)}, bf16[640,128]{1,0:T(8,128)(2,1)}, u32[]{:S(2)}) copy-start(bf16[640,128]{1,0:T(8,128)(2,1)} %param.23) | copy-start | bytes 491524
  20.2 13.6 %copy-start.9 = (bf16[512,128]{1,0:T(8,128)(2,1)S(1)}, bf16[512,128]{1,0:T(8,128)(2,1)}, u32[]{:S(2)}) copy-start(bf16[512,128]{1,0:T(8,128)(2,1)} %param.22) | copy-start | bytes 393220
  20.2 15.0 %copy-start.15 = (s32[1,96]{1,0:T(1,128)S(1)}, s32[1,96]{1,0:T(1,128)}, u32[]{:S(2)}) copy-start(s32[1,96]{1,0:T(1,128)} %param.16) | copy-start | bytes 1156
  20.2 15.0 %copy-start.12 = (s32[1,48]{1,0:T(1,128)S(1)}, s32[1,48]{1,0:T(1,128)}, u32[]{:S(2)}) copy-start(s32[1,48]{1,0:T(1,128)} %param.20) | copy-start | bytes 580
  20.2 15.1 %copy-start.14 = (s32[1,48]{1,0:T(1,128)S(1)}, s32[1,48]{1,0:T(1,128)}, u32[]{:S(2)}) copy-start(s32[1,48]{1,0:T(1,128)} %param.21) | copy-start | bytes 580
  20.2 63.1 %all-to-all-start = ((bf16[64,128,128]{2,1,0:T(8,128)(2,1)}), bf16[64,128,128]{2,1,0:T(8,128)(2,1)}, u32[]{:S(2)}, u32[]{:S(2)}) async-start(bf16[64,128,128]{2,1,0:T(8,128)(2,1)} %gather_fusion), calls=%async_computation | async-start | bytes 4194304 | tf_op jit(solution)/shard_map/all_to_all | solution.py:72
  33.7 100.5 %reduce-scatter.2.cloned.1.call-start = ((), (), s32[]{:S(2)}) async-start(), calls=%async_computation.3 | async-start | bytes 1638400 | tf_op jit(solution)/shard_map/reduce_scatter | solution.py:89
  94.6 6.7 %copy-start.13 = (s32[1,96]{1,0:T(1,128)S(1)}, s32[1,96]{1,0:T(1,128)}, u32[]{:S(2)}) copy-start(s32[1,96]{1,0:T(1,128)} %param.17) | copy-start | bytes 1156
  101.3 5.0 copy-start.11
  105.6 0.7 copy-start.3
  106.5 11.8 %copy-start.6 = (bf16[640,128]{1,0:T(8,128)(2,1)}, bf16[640,128]{1,0:T(8,128)(2,1)S(1)}, u32[]{:S(2)}) copy-start(bf16[640,128]{1,0:T(8,128)(2,1)S(1)} %fusion.15) | copy-start | bytes 491524
  106.5 7.4 %collective-permute-start = (bf16[5,128,128]{2,1,0:T(8,128)(2,1)S(1)}, bf16[5,128,128]{2,1,0:T(8,128)(2,1)S(1)}, u32[]{:S(2)}, u32[]{:S(2)}) collective-permute-start(bf16[5,128,128]{2,1,0:T(8,128)(2,1)S(1)} %bitcast.132), channel_id=1, source_target_pairs={{0,4},{4,8},{8,12},{12,16},{16,20},{20,24},{24,28},{28,32},{32,36}... | collective-permute-start | bytes 491528 | tf_op jit(solution)/shard_map/ppermute | solution.py:12
  111.6 6.6 %collective-permute-start.1 = (bf16[5,128,128]{2,1,0:T(8,128)(2,1)S(1)}, bf16[5,128,128]{2,1,0:T(8,128)(2,1)S(1)}, u32[]{:S(2)}, u32[]{:S(2)}) collective-permute-start(bf16[5,128,128]{2,1,0:T(8,128)(2,1)S(1)} %bitcast.133), channel_id=1, source_target_pairs={{4,0},{8,4},{12,8},{16,12},{20,16},{24,20},{28,24},{32,28},{36,32}... | collective-permute-start | bytes 491528 | tf_op jit(solution)/shard_map/ppermute | solution.py:15
  149.0 12.0 %copy-start.4 = (f32[5,128,128]{2,1,0:T(8,128)S(1)}, f32[5,128,128]{2,1,0:T(8,128)}, u32[]{:S(2)}) copy-start(f32[5,128,128]{2,1,0:T(8,128)} %copy-done.3) | copy-start | bytes 983044
  149.1 10.5 %collective-permute-start.2 = (f32[5,128,128]{2,0,1:T(8,128)S(1)}, f32[5,128,128]{2,0,1:T(8,128)S(1)}, u32[]{:S(2)}, u32[]{:S(2)}) collective-permute-start(f32[5,128,128]{2,0,1:T(8,128)S(1)} %get-tuple-element.8), channel_id=1, source_target_pairs={{4,0},{8,4},{12,8},{16,12},{20,16},{24,20},{28,24},{32,28},{36,32}... | collective-permute-start | bytes 983048 | tf_op jit(solution)/shard_map/ppermute | solution.py:23
  151.0 9.8 %collective-permute-start.3 = (f32[5,128,128]{2,0,1:T(8,128)S(1)}, f32[5,128,128]{2,0,1:T(8,128)S(1)}, u32[]{:S(2)}, u32[]{:S(2)}) collective-permute-start(f32[5,128,128]{2,0,1:T(8,128)S(1)} %get-tuple-element.9), channel_id=1, source_target_pairs={{0,4},{4,8},{8,12},{12,16},{16,20},{20,24},{24,28},{28,32},{32,36}... | collective-permute-start | bytes 983048 | tf_op jit(solution)/shard_map/ppermute | solution.py:23
  186.4 15.2 %copy-start.8 = (bf16[640,128]{1,0:T(8,128)(2,1)S(1)}, bf16[640,128]{1,0:T(8,128)(2,1)}, u32[]{:S(2)}) copy-start(bf16[640,128]{1,0:T(8,128)(2,1)} %get-tuple-element.11) | copy-start | bytes 491524
  186.4 109.6 %all-to-all-start.1 = ((f32[64,128,128]{2,1,0:T(8,128)}), f32[64,128,128]{2,1,0:T(8,128)}, u32[]{:S(2)}, u32[]{:S(2)}) async-start(f32[64,128,128]{2,1,0:T(8,128)} %copy.40), calls=%async_computation.2 | async-start | bytes 8388608 | tf_op jit(solution)/shard_map/all_to_all | solution.py:106
  201.5 298.0 %all-reduce.3.cloned.1.call-start = ((), (), s32[]{:S(2)}) async-start(), calls=%async_computation.4 | async-start | bytes 1015808 | tf_op jit(solution)/shard_map/psum | solution.py:110
  216.2 94.3 %copy-start.2 = (bf16[640,512]{1,0:T(8,128)(2,1)}, bf16[640,512]{1,0:T(8,128)(2,1)S(1)}, u32[]{:S(2)}) copy-start(bf16[640,512]{1,0:T(8,128)(2,1)S(1)} %all_gather.3) | copy-start | bytes 1966084
  315.6 6.4 %copy-start.7 = (bf16[640,128]{1,0:T(8,128)(2,1)S(1)}, bf16[640,128]{1,0:T(8,128)(2,1)}, u32[]{:S(2)}) copy-start(bf16[640,128]{1,0:T(8,128)(2,1)} %copy-done.6) | copy-start | bytes 491524
  315.6 6.4 %copy-start.10 = (bf16[512,128]{1,0:T(8,128)(2,1)S(1)}, bf16[512,128]{1,0:T(8,128)(2,1)}, u32[]{:S(2)}) copy-start(bf16[512,128]{1,0:T(8,128)(2,1)} %param.22) | copy-start | bytes 393220
  315.6 187.2 %copy-start.1 = (bf16[96,128,128]{2,1,0:T(8,128)(2,1)S(1)}, bf16[96,128,128]{2,1,0:T(8,128)(2,1)}, u32[]{:S(2)}) copy-start(bf16[96,128,128]{2,1,0:T(8,128)(2,1)} %param.15) | copy-start | bytes 9437188
Sparse Core Ops, SparseCore 0:
  37.1 26.8 reduce-scatter.1
  322.0 177.4 all-reduce.2
where the time goes:
time: 511 us; the launch traced here: 510 us
  waiting for transfers between devices  313 us (61%)
  local copies, waits for them, and re-layouts  60.7 us (12%)
  matrix products  56 us (11%)
  starting transfers between devices  41.7 us (8%)
  blocking collectives  14.6 us (3%)
  between operations  14.4 us (3%)
  other arithmetic  9.73 us (2%)
    psum x1, waiting for transfers between devices, on_device(): grad_embed, grad_node = lax.psum((grad_embed_part, grad_rows), 'band')  175 us
    all_to_all x1, waiting for transfers between devices, on_device(): lax.all_to_all(grad_received, 'band', split_axis=0, concat_axis=0, tiled=...  78.6 us
    all_to_all x1, waiting for transfers between devices, on_device(): lax.all_to_all(latent[send_list], 'band', split_axis=0, concat_axis=0, ti...  48 us
    all_to_all x1, starting transfers between devices, on_device(): lax.all_to_all(grad_received, 'band', split_axis=0, concat_axis=0, tiled=...  15.1 us
    all_gather x1, blocking collectives, on_device(): shard_part = lax.all_gather(hidden, 'chan', axis=1, tiled=True)  14.6 us
    all_to_all x1, starting transfers between devices, on_device(): lax.all_to_all(latent[send_list], 'band', split_axis=0, concat_axis=0, ti...  13.5 us
    scatter x1, local copies, waits for them, and re-layouts, on_device(): jnp.zeros_like(grad_sent).at[send_list].set(grad_sent)  12.1 us
    dot_general x2, matrix products, collect(): jnp.einsum('pij,pjc->pic', weights, picked, preferred_element_type=jnp.fl...  11.6 us
  transfers between devices with their start and end apart: 8, of which 7 were waited for; matrix products, arithmetic and copies ran while one was open for 8% of the time, Pallas kernels for 0%

commit v1 on v0

v1 whole, which is shorter than its diff:
```python
import jax
import jax.numpy as jnp
from jax import lax
from jax.experimental import pallas as pl
from jax.experimental.pallas import tpu as pltpu
from jax.sharding import PartitionSpec as P

MESH = pl.DeviceIdType.MESH
F32 = jnp.float32
BF = jnp.bfloat16
NB = 64
NX = 4
C_IN = 474
CP = 480
LAT = 512
W = 128
T = NB // NX
EP = 96
PP = 48
MB = 5
MR = MB * W
ER = T * W
NT = 32
CELLS = MB * T


def dot(a, b):
    return jnp.dot(a, b, preferred_element_type=F32)


def slope_of(v, s):
    return s * (1.0 + v * (1.0 - s))


def al(v, m):
    return pl.multiple_of(v, m)


def kernel(
    order, eslot, edest, psrc, pdest, grid, wemb, ecoef, meshin, pcoef, wnode, ograd,
    mesh_out, mesh_grad, gemb, gnode,
    gv, stage, recv, we_all, wtmp, og_all, wn, wr_all, mi, ce, cp,
    wide, cells, a_enc, a_proc, at_proc, gh, slope,
    part, enc_sum, enc_slope_f, rs1, ext, hid_all, hb_out, hb_in, mid, gn_out, gn_in, ge_all, gp,
    gemb_f, gemb_out, rs2, red, ra, sb, rb, fin, fin2,
    lsem, g_s, a_s, a_r, x_s, x_r, h_s, h_r, b_s, b_r, c_s, c_r, t_s, t_r, u_s, u_r,
):
    me = lax.axis_index("band")
    x = lax.axis_index("chan")
    core = lax.rem(me, 2)
    chip = lax.div(me, 2)
    mine = pl.ds(al(x * W, W), W)

    def to_band(src, dst, ss, rs, band):
        return pltpu.make_async_remote_copy(src, dst, ss, rs, device_id={"band": band}, device_id_type=MESH)

    def to_chan(src, dst, ss, rs, chan):
        return pltpu.make_async_remote_copy(src, dst, ss, rs, device_id={"chan": chan}, device_id_type=MESH)

    def peer(dx):
        return lax.rem(x + dx, NX)

    def cols(c):
        return pl.ds(al(c * W, W), W)

    def rows_of(c):
        return pl.ds(al(c * W, W), W)

    def load_block(b):
        return pltpu.make_async_copy(grid.at[:, cols(b)], gv.at[b], g_s.at[b])

    def load_start(b, _):
        load_block(b).start()
        return 0

    lax.fori_loop(0, NB, load_start, 0)
    load_wemb = pltpu.make_async_copy(wemb, wtmp, lsem.at[1])
    load_og = pltpu.make_async_copy(ograd, og_all.at[:, mine], lsem.at[2])
    load_wn = pltpu.make_async_copy(wnode, wn, lsem.at[3])
    load_mi = pltpu.make_async_copy(meshin, mi, lsem.at[4])
    load_ce = pltpu.make_async_copy(ecoef, ce, lsem.at[5])
    load_cp = pltpu.make_async_copy(pcoef, cp, lsem.at[6])
    load_wemb.start()
    load_og.start()
    load_wn.start()

    barrier = pltpu.get_barrier_semaphore()

    def greet(j, _):
        pl.semaphore_signal(barrier, inc=1, device_id={"band": lax.rem(me + j, NB)}, device_id_type=MESH)
        return 0

    lax.fori_loop(1, NB, greet, 0)
    for dx in range(1, NX):
        pl.semaphore_signal(barrier, inc=1, device_id={"chan": peer(dx)}, device_id_type=MESH)

    stage[:, CP - 16 :, :] = jnp.zeros((T, 16, W), BF)

    def load_wait(b, _):
        load_block(b).wait()
        return 0

    lax.fori_loop(0, NB, load_wait, 0)
    pl.semaphore_wait(barrier, NB - 1 + NX - 1)

    def grid_copy(t):
        d = lax.rem(me + x + NX * t, NB)
        return to_band(stage.at[t], recv.at[:, cols(t)], a_s.at[t], a_r.at[t], d)

    def send_grid(t, _):
        d = lax.rem(me + x + NX * t, NB)
        stage[t, :C_IN, :] = gv[order[0, d]]

        @pl.when(x + t != 0)
        def _():
            grid_copy(t).start()

        return 0

    lax.fori_loop(0, T, send_grid, 0)
    load_mi.start()
    load_ce.start()
    load_cp.start()

    @pl.when(x == 0)
    def _():
        recv[:, 0:W] = stage[0]

    load_wemb.wait()
    we_all[mine, CP - W : CP] = jnp.zeros((W, W), BF)
    we_all[mine, :C_IN] = wtmp[...].astype(F32).T.astype(BF)
    load_og.wait()
    load_wn.wait()
    wr_all[:, mine] = wn[mine, :]

    def early(dx):
        p = peer(dx)
        return (
            to_chan(we_all.at[mine, :], we_all.at[mine, :], x_s.at[0, dx], x_r.at[0, dx], p),
            to_chan(og_all.at[:, mine], og_all.at[:, mine], x_s.at[1, dx], x_r.at[1, dx], p),
            to_chan(wn.at[rows_of(p), :], wr_all.at[:, mine], x_s.at[2, dx], x_r.at[2, dx], p),
        )

    for dx in range(1, NX):
        for c in early(dx):
            c.start()

    def sum_cells(coef, pairs, hits):
        wide[0 : pairs * W, :] = coef[...].astype(F32)
        pick = jnp.where(hits, 1.0, 0.0).astype(BF)

        def one(i, _):
            line = wide[pl.ds(i, pairs, stride=W), :].astype(BF)
            cells[pl.ds(i, CELLS, stride=W), :] = dot(pick, line)
            return 0

        lax.fori_loop(0, W, one, 0, unroll=4)

    def cell_ids(pairs):
        cell = lax.broadcasted_iota(jnp.int32, (CELLS, pairs), 0)
        return lax.shift_right_logical(cell, 4), lax.bitwise_and(cell, T - 1)

    load_ce.wait()
    cell_m, cell_t = cell_ids(EP)
    cell_slot = lax.bitwise_and(me - x - NX * cell_t + 2 * NB, NB - 1)
    sum_cells(ce, EP, (edest[...] == cell_m) & (eslot[...] == cell_slot))

    def enc_cells(t, _):
        for m in range(MB):
            a_enc[m * W : (m + 1) * W, cols(t)] = cells[rows_of(m * T + t), :].astype(BF)
        return 0

    lax.fori_loop(0, T, enc_cells, 0)

    load_cp.wait()
    cell_m, cell_s = cell_ids(PP)
    sum_cells(cp, PP, (pdest[...] == cell_m) & (psrc[...] == cell_s))

    def proc_cells(s, _):
        for m in range(MB):
            block = cells[rows_of(m * T + s), :]
            a_proc[m * W : (m + 1) * W, cols(s)] = block.astype(BF)
            at_proc[rows_of(s), m * W : (m + 1) * W] = block.T.astype(BF)
        return 0

    lax.fori_loop(0, 3 * MB, proc_cells, 0)

    for dx in range(1, NX):
        for c in early(dx):
            c.wait_recv()
    gh[...] = lax.dot_general(og_all[...], wr_all[...], (((1,), (1,)), ((), ())), preferred_element_type=F32)

    def dot_nt(a, b):
        return lax.dot_general(a, b, (((1,), (1,)), ((), ())), preferred_element_type=F32)

    enc_sum[...] = jnp.zeros((MR, LAT), F32)

    def embed(u, _):
        for v in range(2):
            t = 2 * u + v

            @pl.when(x + t != 0)
            def _():
                grid_copy(t).wait_recv()

        here = pl.ds(al(u * 2 * W, 2 * W), 2 * W)
        pre = dot(we_all[...], recv[:, here])
        sig = jax.nn.sigmoid(pre)
        latent = (pre * sig).astype(BF)
        slope[:, here] = slope_of(pre, sig)
        enc_sum[...] += dot_nt(a_enc[:, here], latent)
        return 0

    lax.fori_loop(0, T // 2, embed, 0)

    half = lax.div(x, 2)
    away = 1 - half
    twin = x + 1 - 2 * lax.rem(x, 2)
    far = (2 * away, 2 * away + 1)

    def two(h):
        return pl.ds(al(h * 2 * W, 2 * W), 2 * W)

    def enc_copy(c):
        return to_chan(part.at[:, cols(c)], rs1.at[x], c_s.at[0, c], c_r.at[0, x], c)

    part[:, two(away)] = enc_sum[:, two(away)].astype(BF)
    for c in far:
        enc_copy(c).start()
    part[:, cols(twin)] = enc_sum[:, cols(twin)].astype(BF)
    enc_copy(twin).start()

    load_mi.wait()
    enc_pre = enc_sum[:, mine]
    for dx in range(1, NX):
        p = peer(dx)
        to_chan(part.at[:, cols(p)], rs1.at[p], c_s.at[0, p], c_r.at[0, p], p).wait_recv()
        enc_pre = enc_pre + rs1[p].astype(F32)
    enc_sig = jax.nn.sigmoid(enc_pre)
    mesh_one = (mi[...].astype(F32) + enc_pre * enc_sig).astype(BF)
    enc_slope = slope_of(enc_pre, enc_sig)
    enc_slope_f[...] = enc_slope

    ext[MR : 2 * MR, :] = mesh_one
    has_low = me > 0
    has_high = me < NB - 1
    low = lax.rem(me + NB - 1, NB)
    high = lax.rem(me + 1, NB)
    own_ext = ext.at[MR : 2 * MR, :]
    halo_up = to_band(own_ext, ext.at[0:MR, :], h_s.at[0], h_r.at[0], high)
    halo_down = to_band(own_ext, ext.at[2 * MR : 3 * MR, :], h_s.at[1], h_r.at[1], low)
    pl.when(has_high)(halo_up.start)
    pl.when(has_low)(halo_down.start)
    mid[...] = dot(a_proc[:, MR : 2 * MR], mesh_one)

    @pl.when(me == 0)
    def _():
        ext[0:MR, :] = jnp.zeros((MR, W), BF)

    @pl.when(me == NB - 1)
    def _():
        ext[2 * MR : 3 * MR, :] = jnp.zeros((MR, W), BF)

    pl.when(has_low)(halo_up.wait_recv)
    pl.when(has_high)(halo_down.wait_recv)
    proc_pre = (
        mid[...]
        + dot(a_proc[:, 0:MR], ext[0:MR, :])
        + dot(a_proc[:, 2 * MR : 3 * MR], ext[2 * MR : 3 * MR, :])
    )
    proc_sig = jax.nn.sigmoid(proc_pre)
    hidden = (proc_pre * proc_sig).astype(BF)
    hid_all[:, mine] = hidden

    def hid_copy(c):
        return to_chan(hid_all.at[:, mine], hid_all.at[:, mine], c_s.at[1, c], c_r.at[1, x], c)

    for dx in range(1, NX):
        hid_copy(peer(dx)).start()
    grad_proc = (gh[...] * slope_of(proc_pre, proc_sig)).astype(BF)

    hb_out[0] = dot(at_proc[0:MR, :], grad_proc).astype(BF)
    back_down = to_band(hb_out.at[0], hb_in.at[0], b_s.at[0], b_r.at[0], low)
    pl.when(has_low)(back_down.start)
    hb_out[1] = dot(at_proc[2 * MR : 3 * MR, :], grad_proc).astype(BF)
    back_up = to_band(hb_out.at[1], hb_in.at[1], b_s.at[1], b_r.at[1], high)
    pl.when(has_high)(back_up.start)
    mid[...] = dot(at_proc[MR : 2 * MR, :], grad_proc) + og_all[:, mine].astype(F32)

    gn_out[...] = dot(hidden.astype(F32).T.astype(BF), og_all[...])
    gn_in[mine, :] = gn_out[:, mine]

    def gn_copy(c):
        return to_chan(gn_out.at[:, cols(c)], gn_in.at[mine, :], c_s.at[2, c], c_r.at[2, x], c)

    for dx in range(1, NX):
        gn_copy(peer(dx)).start()

    @pl.when(me == NB - 1)
    def _():
        hb_in[0] = jnp.zeros((MR, W), BF)

    @pl.when(me == 0)
    def _():
        hb_in[1] = jnp.zeros((MR, W), BF)

    pl.when(has_high)(back_down.wait_recv)
    pl.when(has_low)(back_up.wait_recv)
    total = mid[...] + hb_in[0].astype(F32) + hb_in[1].astype(F32)
    mesh_grad[...] = total
    ge_all[mine, :] = (total * enc_slope_f[...]).T.astype(BF)

    def ge_copy(c):
        return to_chan(ge_all.at[mine, :], ge_all.at[mine, :], c_s.at[3, c], c_r.at[3, x], c)

    def ge_wait(c):
        to_chan(ge_all.at[rows_of(c), :], ge_all.at[rows_of(c), :], c_s.at[3, c], c_r.at[3, c], c).wait_recv()

    for dx in range(1, NX):
        ge_copy(peer(dx)).start()

    for dx in range(1, NX):
        p = peer(dx)
        to_chan(hid_all.at[:, cols(p)], hid_all.at[:, cols(p)], c_s.at[1, p], c_r.at[1, p], p).wait_recv()
    mesh_out[...] = (ext[MR : 2 * MR, :].astype(F32) + dot(hid_all[...], wn[...])).astype(BF)

    def back(h):
        def piece(t, _):
            here = pl.ds(al(t * 512, 512), 512)
            msg = dot(ge_all[two(h), :], a_enc[:, here])
            gp[:, here] = (msg * slope[two(h), here]).astype(BF)
            return 0

        lax.fori_loop(0, ER // 512, piece, 0)
        gemb_f[...] = dot_nt(recv[...], gp[...])

    def ge2_copy(c):
        return to_chan(gemb_out.at[:, cols(c)], rs2.at[x], c_s.at[4, c], c_r.at[4, x], c)

    ge_wait(twin)
    back(half)
    red[0, 0:CP, :] = gemb_f[:, pl.ds(al(lax.rem(x, 2) * W, W), W)]
    red[0, CP:, :] = jnp.zeros((LAT - CP, W), F32)
    gemb_out[:, two(half)] = gemb_f[...].astype(BF)
    ge2_copy(twin).start()
    for c in far:
        ge_wait(c)
    back(away)
    gemb_out[:, two(away)] = gemb_f[...].astype(BF)
    for c in far:
        ge2_copy(c).start()

    for dx in range(1, NX):
        p = peer(dx)
        prow = pl.ds(al(p * W, W), W)
        to_chan(gn_out.at[:, cols(p)], gn_in.at[prow, :], c_s.at[2, p], c_r.at[2, p], p).wait_recv()
    red[1] = gn_in[...]
    for dx in range(1, NX):
        p = peer(dx)
        to_chan(gemb_out.at[:, cols(p)], rs2.at[p], c_s.at[4, p], c_r.at[4, p], p).wait_recv()
    red[0, 0:CP, :] += rs2[peer(1)].astype(F32) + rs2[peer(2)].astype(F32) + rs2[peer(3)].astype(F32)

    sibling = me + 1 - 2 * core
    keep = pl.ds(al(core * 256, 256), 256)
    give = pl.ds(al((1 - core) * 256, 256), 256)
    swap = to_band(red.at[:, give, :], ra, t_s.at[0], t_r.at[0], sibling)
    swap.start()
    swap.wait_recv()
    sb[...] = (red[:, keep, :] + ra[...]).astype(BF).reshape(NT, 16, W)

    def scatter_copy(j):
        d = lax.rem(chip + j, NT)
        return to_band(sb.at[d], rb.at[chip], u_s.at[0, j], u_r.at[0, j], 2 * d + core)

    def scatter(j, _):
        scatter_copy(j).start()
        return 0

    lax.fori_loop(1, NT, scatter, 0)
    rb[chip] = sb[chip]

    def scatter_wait(j, _):
        scatter_copy(j).wait_recv()
        return 0

    lax.fori_loop(1, NT, scatter_wait, 0)
    fin[chip] = jnp.sum(rb[...].astype(F32), axis=0).astype(BF)

    def gather_copy(j):
        d = lax.rem(chip + j, NT)
        return to_band(fin.at[chip], fin.at[chip], u_s.at[1, j], u_r.at[1, j], 2 * d + core)

    def gather(j, _):
        gather_copy(j).start()
        return 0

    lax.fori_loop(1, NT, gather, 0)

    def gather_wait(j, _):
        s = lax.rem(chip - j + NT, NT)
        to_band(fin.at[s], fin.at[s], u_s.at[1, j], u_r.at[1, j], 2 * s + core).wait_recv()
        return 0

    lax.fori_loop(1, NT, gather_wait, 0)
    swap_back = to_band(fin, fin2, t_s.at[1], t_r.at[1], sibling)
    swap_back.start()
    swap_back.wait_recv()
    own = fin[...].reshape(2, 256, W).astype(F32)
    other = fin2[...].reshape(2, 256, W).astype(F32)
    gnode[keep, :] = own[1]
    gnode[give, :] = other[1]

    @pl.when(core == 0)
    def _():
        gemb[0:256, :] = own[0]
        gemb[256:C_IN, :] = other[0][: C_IN - 256]

    @pl.when(core == 1)
    def _():
        gemb[0:256, :] = other[0]
        gemb[256:C_IN, :] = own[0][: C_IN - 256]

    def sent_grid(t, _):
        @pl.when(x + t != 0)
        def _():
            grid_copy(t).wait_send()

        return 0

    lax.fori_loop(0, T, sent_grid, 0)
    for dx in range(1, NX):
        p = peer(dx)
        for c in early(dx):
            c.wait_send()
        for f in (enc_copy, hid_copy, gn_copy, ge_copy, ge2_copy):
            f(p).wait_send()
    pl.when(has_high)(halo_up.wait_send)
    pl.when(has_low)(halo_down.wait_send)
    pl.when(has_low)(back_down.wait_send)
    pl.when(has_high)(back_up.wait_send)
    swap.wait_send()
    swap_back.wait_send()

    def sent_small(j, _):
        scatter_copy(j).wait_send()
        gather_copy(j).wait_send()
        return 0

    lax.fori_loop(1, NT, sent_small, 0)


def on_device(
    grid_in, w_embed, send_order, enc_coef, enc_slot, enc_dest, mesh_in, proc_coef, proc_src, proc_dest, w_node, out_grad
):
    smem = pl.BlockSpec(memory_space=pltpu.SMEM)
    hbm = pl.BlockSpec(memory_space=pl.ANY)
    vmem = pl.BlockSpec(memory_space=pltpu.VMEM)
    V = pltpu.VMEM
    dma = pltpu.SemaphoreType.DMA
    return pl.pallas_call(
        kernel,
        out_shape=(
            jax.ShapeDtypeStruct((MR, W), BF),
            jax.ShapeDtypeStruct((MR, W), F32),
            jax.ShapeDtypeStruct((C_IN, W), F32),
            jax.ShapeDtypeStruct((LAT, W), F32),
        ),
        in_specs=[smem] + [vmem] * 4 + [hbm] * 7,
        out_specs=(vmem,) * 4,
        scratch_shapes=[
            V((NB, C_IN, W), BF),
            V((T, CP, W), BF),
            V((CP, ER), BF),
            V((LAT, CP), BF),
            V((C_IN, W), BF),
            V((MR, LAT), BF),
            V((LAT, W), BF),
            V((W, LAT), BF),
            V((MR, W), BF),
            V((EP * W, W), BF),
            V((PP * W, W), BF),
            V((EP * W, W), F32),
            V((CELLS * W, W), F32),
            V((MR, ER), BF),
            V((MR, 3 * MR), BF),
            V((3 * MR, MR), BF),
            V((MR, W), F32),
            V((LAT, ER), F32),
            V((MR, LAT), BF),
            V((MR, LAT), F32),
            V((MR, W), F32),
            V((NX, MR, W), BF),
            V((3 * MR, W), BF),
            V((MR, LAT), BF),
            V((2, MR, W), BF),
            V((2, MR, W), BF),
            V((MR, W), F32),
            V((W, LAT), F32),
            V((LAT, W), F32),
            V((LAT, MR), BF),
            V((2 * W, ER), BF),
            V((CP, 2 * W), F32),
            V((CP, LAT), BF),
            V((NX, CP, W), BF),
            V((2, 512, W), F32),
            V((2, 256, W), F32),
            V((NT, 16, W), BF),
            V((NT, 16, W), BF),
            V((NT, 16, W), BF),
            V((NT, 16, W), BF),
            dma((7,)),
            dma((NB,)),
            dma((T,)), dma((T,)),
            dma((3, NX)), dma((3, NX)),
            dma((2,)), dma((2,)),
            dma((2,)), dma((2,)),
            dma((5, NX)), dma((5, NX)),
            dma((2,)), dma((2,)),
            dma((2, NT)), dma((2, NT)),
        ],
        compiler_params=pltpu.CompilerParams(
            collective_id=0, has_side_effects=True, vmem_limit_bytes=60 << 20
        ),
    )(
        send_order, enc_slot, enc_dest, proc_src, proc_dest,
        grid_in.T, w_embed, enc_coef.reshape(EP * W, W), mesh_in,
        proc_coef.reshape(PP * W, W), w_node, out_grad,
    )


def solution(mesh):
    return jax.shard_map(
        on_device,
        mesh=mesh,
        in_specs=(
            P("band", None),
            P(None, "chan"),
            P("band", None),
            P("band", None, None),
            P("band", None),
            P("band", None),
            P("band", "chan"),
            P("band", None, None),
            P("band", None),
            P("band", None),
            P(None, "chan"),
            P("band", "chan"),
        ),
        out_specs=(P("band", "chan"), P("band", "chan"), P(None, "chan"), P(None, "chan")),
        check_vma=False,
    )
```

time: 511 us -> 131 us (0.26)
  waiting for transfers between devices: 313 us -> 0 us
  Pallas kernels: 0 us -> 124 us
  matrix products: 56 us -> 0 us
  local copies, waits for them, and re-layouts: 60.7 us -> 6.63 us
  starting transfers between devices: 41.7 us -> 0 us
  blocking collectives: 14.6 us -> 0 us
  between operations: 14.4 us -> 0.65 us
  other arithmetic: 9.73 us -> 0 us
    psum x1 -> x0, waiting for transfers between devices: 175 us -> none  [on_device(): grad_embed, grad_node = lax.psum((grad_embed_part, grad_rows), 'band')]
    all_to_all x2 -> x0, waiting for transfers between devices: 127 us -> none  [the longest x1 78.6 us: on_device(): lax.all_to_all(grad_received, 'band', split_axis=0, concat_axis=0, tiled=...]
    pallas_call x0 -> x1, Pallas kernels: none -> 124 us  [on_device(): pl.pallas_call(kernel, out_shape=(jax.ShapeDtypeStruct((MR, W), BF), jax....]
    dot_general x13 -> x0, matrix products: 56 us -> none  [the longest x2 11.6 us: collect(): jnp.einsum('pij,pjc->pic', weights, picked, preferred_element_type=jnp.fl...]
    all_to_all x2 -> x0, starting transfers between devices: 28.6 us -> none  [the longest x1 15.1 us: on_device(): lax.all_to_all(grad_received, 'band', split_axis=0, concat_axis=0, tiled=...]
    dot_general x7 -> x0, local copies, waits for them, and re-layouts: 25.9 us -> none  [the longest x2 10.3 us: collect(): jnp.einsum('pij,pjc->pic', weights, picked, preferred_element_type=jnp.fl...]
    gather x5 -> x0, local copies, waits for them, and re-layouts: 15.9 us -> none  [the longest x2 7.37 us: collect(): picked = source[source_ids]]
    all_gather x1 -> x0, blocking collectives: 14.6 us -> none  [on_device(): shard_part = lax.all_gather(hidden, 'chan', axis=1, tiled=True)]
  transfers between devices with their start and end apart: 8 -> 0, of which waited for: 7 -> 0; matrix products, arithmetic and copies ran while one was open for 8% -> 0% of each run, Pallas kernels for 0% -> 0%
where the time goes in v1:
time: 131 us
  Pallas kernels  124 us (95%)
  local copies, waits for them, and re-layouts  6.63 us (5%)
    pallas_call x1, Pallas kernels, on_device(): pl.pallas_call(kernel, out_shape=(jax.ShapeDtypeStruct((MR, W), BF), jax....  124 us
    unnamed x4, local copies, waits for them, and re-layouts  6.63 us

profile of v1, /device:TPU:1, one launch (start us, length us, event | category | flops | bytes accessed | tf_op | source)
XLA Modules:
  0.0 131.3 jit_solution(8774856777719865061)
XLA Ops:
  0.6 124.0 %shard_map.147 = (bf16[640,128]{1,0:T(8,128)(2,1)}, f32[640,128]{1,0:T(8,128)}, f32[474,128]{1,0:T(8,128)}, f32[512,128]{1,0:T(8,128)}) custom-call(s32[1,64]{1,0:T(1,128)} %order.1, s32[1,96]{1,0:T(1,128)} %eslot.1, s32[1,96]{1,0:T(1,128)} %edest.1, s32[1,48]{1,0:T(1,128)} %psrc.1, s32[1,48]{1,0:T(1,128)} %pdest.1, bf16[474,8192]{1,0:T(8,128)(2,1)} %bitcast.3, ...), custom_call_target="tpu_custom_call" | custom-call | tf_op jit(solution)/shard_map/pallas_call | solution.py:460
  124.6 1.6 %copy.20 = bf16[640,128]{1,0:T(8,128)(2,1)} copy(bf16[640,128]{1,0:T(8,128)(2,1)} %get-tuple-element.8) | data formatting | bytes 327680
  126.2 1.7 %copy.21 = f32[640,128]{1,0:T(8,128)} copy(f32[640,128]{1,0:T(8,128)} %get-tuple-element.9) | data formatting | bytes 655360
  128.0 1.7 %copy.22 = f32[474,128]{1,0:T(8,128)} copy(f32[474,128]{1,0:T(8,128)} %get-tuple-element.10) | data formatting | bytes 485376
  129.6 1.7 %copy.23 = f32[512,128]{1,0:T(8,128)} copy(f32[512,128]{1,0:T(8,128)} %get-tuple-element.11) | data formatting | bytes 524288

commit v2 on v1

v2 whole, which is shorter than its diff:
```python
import jax
import jax.numpy as jnp
from jax import lax
from jax.experimental import pallas as pl
from jax.experimental.pallas import tpu as pltpu
from jax.sharding import PartitionSpec as P

MESH = pl.DeviceIdType.MESH
F32 = jnp.float32
BF = jnp.bfloat16
NB = 64
NX = 4
C_IN = 474
CP = 480
LAT = 512
W = 128
T = NB // NX
EP = 96
PP = 48
MB = 5
MR = MB * W
ER = T * W
CELLS = MB * T
LATE = 4
LATE_CELLS = MB * NX * LATE
FIRST = 4
ZS = 8
YS = 4
ZR = 32
HALF = CP // 2


def dot(a, b):
    return jnp.dot(a, b, preferred_element_type=F32)


def slope_of(v, s):
    return s * (1.0 + v * (1.0 - s))


def al(v, m):
    return pl.multiple_of(v, m)


def finish(out_in, grad_in, fin, fin2, node_fin, node_fin2, mesh_out, mesh_grad, gemb, gnode):
    core = lax.rem(lax.axis_index("band"), 2)
    mesh_out[...] = out_in[...]
    mesh_grad[...] = grad_in[...]
    gnode[pl.ds(al(core * 256, 256), 256), :] = node_fin[...].reshape(256, W)
    gnode[pl.ds(al((1 - core) * 256, 256), 256), :] = node_fin2[...].reshape(256, W)

    def write(low, high):
        gemb[0:HALF, :] = low[...].reshape(256, W)[:HALF].astype(F32)
        gemb[HALF:C_IN, :] = high[...].reshape(256, W)[: C_IN - HALF].astype(F32)

    @pl.when(core == 0)
    def _():
        write(fin, fin2)

    @pl.when(core == 1)
    def _():
        write(fin2, fin)


def kernel(
    order, eslot, edest, psrc, pdest, grid, wemb, ecoef, meshin, pcoef, wnode, ograd,
    mesh_out, mesh_grad, fin_out, fin2_out, node_out, node2_out,
    flat, flat_last, blocks, stage, recv, we_all, wtmp, og_all, wn, wr_all, mi, ce,
    wide, cells, a_enc, a_late, a_proc, at_proc, gh, slope,
    part, enc_sum, enc_slope_f, rs1, lat_out, lat_in, ext, hid_all, hb_out, hb_in, mid, gn_out, gn_in, ge_all, gp,
    half_f, half_out, half_in, gemb_out, rs2, node_in, pieces_e, pieces_n, landed_e, landed_n, by_y, fin_e, fin_e2, fin_n, fin_n2, mo, mg,
    lsem, g_s, f_s, f_r, a_s, a_r, x_s, x_r, h_s, h_r, b_s, b_r, c_s, c_r, t_s, t_r, u_s, u_r, v_s, v_r, l_s, l_r,
):
    me = lax.axis_index("band")
    x = lax.axis_index("chan")
    core = lax.rem(me, 2)
    chip = lax.div(me, 2)
    mine = pl.ds(al(x * W, W), W)

    def to_band(src, dst, ss, rs, band):
        return pltpu.make_async_remote_copy(src, dst, ss, rs, device_id={"band": band}, device_id_type=MESH)

    def to_chan(src, dst, ss, rs, chan):
        return pltpu.make_async_remote_copy(src, dst, ss, rs, device_id={"chan": chan}, device_id_type=MESH)

    def peer(dx):
        return lax.rem(x + dx, NX)

    def cols(c):
        return pl.ds(al(c * W, W), W)

    def rows_of(c):
        return pl.ds(al(c * W, W), W)

    steps = ((0, 128), (128, 256), (256, 384), (384, C_IN))
    load_grid = [
        pltpu.make_async_copy(grid.at[a:b, :], flat_last if i == 3 else flat.at[i % 2], g_s.at[i])
        for i, (a, b) in enumerate(steps)
    ]
    for i in (0, 1, 3):
        load_grid[i].start()
    load_wemb = pltpu.make_async_copy(wemb, wtmp, lsem.at[1])
    load_og = pltpu.make_async_copy(ograd, og_all.at[:, mine], lsem.at[2])
    load_wn = pltpu.make_async_copy(wnode, wn, lsem.at[3])
    load_mi = pltpu.make_async_copy(meshin, mi, lsem.at[4])
    load_ce = pltpu.make_async_copy(ecoef, ce, lsem.at[5])
    cp = ce.at[0 : PP * W, :]
    load_cp = pltpu.make_async_copy(pcoef, cp, lsem.at[6])
    load_wemb.start()
    load_og.start()
    load_wn.start()

    barrier = pltpu.get_barrier_semaphore()

    def greet(band):
        pl.semaphore_signal(barrier, inc=1, device_id={"band": band}, device_id_type=MESH)

    z_here = lax.div(me, 8)
    y_here = lax.rem(chip, YS)
    has_low = me > 0
    has_high = me < NB - 1
    low = lax.rem(me + NB - 1, NB)
    high = lax.rem(me + 1, NB)
    sibling = me + 1 - 2 * core

    def at_z(j):
        return lax.rem(me + 8 * j, NB)

    def at_y(j):
        return z_here * 8 + lax.rem(y_here + j, YS) * 2 + core

    def greet_source(t, _):
        @pl.when(x + t != 0)
        def _():
            greet(lax.rem(me - x - NX * t + 2 * NB, NB))

        return 0

    lax.fori_loop(0, T, greet_source, 0)
    pl.when(has_low)(lambda: greet(low))
    pl.when(has_high)(lambda: greet(high))
    greet(sibling)
    for j in range(1, ZS):
        greet(at_z(j))
    for j in range(1, YS):
        greet(at_y(j))
    for dx in range(1, NX):
        pl.semaphore_signal(barrier, inc=1, device_id={"chan": peer(dx)}, device_id_type=MESH)
    greetings = T + 2 + 1 + ZS - 1 + YS - 1 + NX - 1
    absent = jnp.where(x == 0, 1, 0) + jnp.where(me == 0, 1, 0) + jnp.where(me == NB - 1, 1, 0)

    stage[:, CP - 16 :, :] = jnp.zeros((T, 16, W), BF)
    def band_of(t):
        return lax.rem(me + x + NX * t, NB)

    def first_copy(t):
        rows = pl.ds(0, W)
        return to_band(stage.at[t, rows, :], recv.at[rows, cols(t)], f_s.at[t], f_r.at[t], band_of(t))

    def rest_copy(t):
        rows = pl.ds(W, CP - W)
        return to_band(stage.at[t, rows, :], recv.at[rows, cols(t)], a_s.at[t], a_r.at[t], band_of(t))

    def grid_copy(t):
        return to_band(stage.at[t], recv.at[:, cols(t)], a_s.at[t], a_r.at[t], band_of(t))

    def over_slots(lo, hi, body):
        def one(t, _):
            pl.when(x + t != 0)(lambda: body(t))
            return 0

        lax.fori_loop(lo, hi, one, 0)

    for i, (a, b) in enumerate(steps):
        load_grid[i].wait()

        def by_block(k, _, i=i, n=b - a):
            blocks[k, 0:n, :] = flat_last[:, cols(k)] if i == 3 else flat[i % 2, :, cols(k)]
            return 0

        lax.fori_loop(0, NB, by_block, 0, unroll=4)
        if i == 0:
            load_grid[2].start()

        def to_stage(t, _, a=a, b=b):
            stage[t, a:b, :] = blocks[order[0, band_of(t)], 0 : b - a, :]
            return 0

        lax.fori_loop(0, T, to_stage, 0, unroll=2)
        if i == 0:
            pl.semaphore_wait(barrier, greetings - absent)
            over_slots(0, FIRST, lambda t: first_copy(t).start())
    over_slots(0, FIRST, lambda t: rest_copy(t).start())
    over_slots(FIRST, T - LATE, lambda t: grid_copy(t).start())
    load_mi.start()
    load_ce.start()

    @pl.when(x == 0)
    def _():
        recv[:, 0:W] = stage[0]

    load_wemb.wait()
    we_all[mine, CP - W : CP] = jnp.zeros((W, W), BF)
    we_all[mine, :C_IN] = wtmp[...].astype(F32).T.astype(BF)
    load_og.wait()
    load_wn.wait()
    wr_all[:, mine] = wn[mine, :]

    def early(dx):
        p = peer(dx)
        return (
            to_chan(we_all.at[mine, :], we_all.at[mine, :], x_s.at[0, dx], x_r.at[0, dx], p),
            to_chan(og_all.at[:, mine], og_all.at[:, mine], x_s.at[1, dx], x_r.at[1, dx], p),
            to_chan(wn.at[rows_of(p), :], wr_all.at[:, mine], x_s.at[2, dx], x_r.at[2, dx], p),
        )

    for dx in range(1, NX):
        for c in early(dx):
            c.start()

    def sum_cells(coef, pairs, count, hits):
        wide[0 : pairs * W, :] = coef[...].astype(F32)
        pick = jnp.where(hits, 1.0, 0.0).astype(BF)

        def one(i, _):
            line = wide[pl.ds(i, pairs, stride=W), :].astype(BF)
            cells[pl.ds(i, count, stride=W), :] = dot(pick, line)
            return 0

        lax.fori_loop(0, W, one, 0, unroll=4)

    def cell_ids(pairs):
        cell = lax.broadcasted_iota(jnp.int32, (CELLS, pairs), 0)
        return lax.shift_right_logical(cell, 4), lax.bitwise_and(cell, T - 1)

    load_ce.wait()
    cell = lax.broadcasted_iota(jnp.int32, (CELLS + LATE_CELLS, EP), 0)
    tail = cell - CELLS
    own_group = cell < CELLS
    cell_m = jnp.where(own_group, lax.shift_right_logical(cell, 4), lax.shift_right_arithmetic(tail, 4))
    cell_t = jnp.where(own_group, lax.bitwise_and(cell, T - 1), T - LATE + lax.bitwise_and(tail, LATE - 1))
    cell_x = jnp.where(own_group, x, lax.bitwise_and(lax.shift_right_arithmetic(tail, 2), NX - 1))
    cell_slot = lax.bitwise_and(me - cell_x - NX * cell_t + 2 * NB, NB - 1)
    sum_cells(ce, EP, CELLS + LATE_CELLS, (edest[...] == cell_m) & (eslot[...] == cell_slot))

    load_cp.start()

    def enc_cells(t, _):
        for m in range(MB):
            a_enc[m * W : (m + 1) * W, cols(t)] = cells[rows_of(m * T + t), :].astype(BF)
        return 0

    lax.fori_loop(0, T, enc_cells, 0)

    def late_cells(t, _):
        for m in range(MB):
            a_late[m * W : (m + 1) * W, cols(t)] = cells[rows_of(CELLS + m * NX * LATE + t), :].astype(BF)
        return 0

    lax.fori_loop(0, NX * LATE, late_cells, 0)

    load_cp.wait()
    cell_m, cell_s = cell_ids(PP)
    sum_cells(cp, PP, CELLS, (pdest[...] == cell_m) & (psrc[...] == cell_s))

    def proc_cells(s, _):
        for m in range(MB):
            block = cells[rows_of(m * T + s), :]
            a_proc[m * W : (m + 1) * W, cols(s)] = block.astype(BF)
            at_proc[rows_of(s), m * W : (m + 1) * W] = block.T.astype(BF)
        return 0

    lax.fori_loop(0, 3 * MB, proc_cells, 0)

    for dx in range(1, NX):
        for c in early(dx):
            c.wait_recv()
    gh[...] = lax.dot_general(og_all[...], wr_all[...], (((1,), (1,)), ((), ())), preferred_element_type=F32)

    def sent_first(t):
        first_copy(t).wait_send()
        rest_copy(t).wait_send()

    over_slots(0, FIRST, sent_first)
    over_slots(FIRST, T - LATE, lambda t: grid_copy(t).wait_send())
    over_slots(T - LATE, T, lambda t: grid_copy(t).start())

    def dot_nt(a, b):
        return lax.dot_general(a, b, (((1,), (1,)), ((), ())), preferred_element_type=F32)

    enc_sum[...] = jnp.zeros((MR, LAT), F32)

    def embed(u):
        here = pl.ds(al(u * 2 * W, 2 * W), 2 * W)
        pre = dot(we_all[...], recv[:, here])
        sig = jax.nn.sigmoid(pre)
        slope[:, here] = slope_of(pre, sig)
        return (pre * sig).astype(BF), here

    def embed_sum(u, _):
        latent, here = embed(u)
        enc_sum[...] += dot_nt(a_enc[:, here], latent)
        return 0

    def first_slots(u, _):
        def arrive(t):
            first_copy(t).wait_recv()
            rest_copy(t).wait_recv()

        over_slots(2 * u, 2 * u + 2, arrive)
        return embed_sum(u, 0)

    def other_slots(u, _):
        over_slots(2 * u, 2 * u + 2, lambda t: grid_copy(t).wait_recv())
        return embed_sum(u, 0)

    lax.fori_loop(0, FIRST // 2, first_slots, 0)
    lax.fori_loop(FIRST // 2, (T - LATE) // 2, other_slots, 0)

    half = lax.div(x, 2)
    away = 1 - half
    twin = x + 1 - 2 * lax.rem(x, 2)
    far = (2 * away, 2 * away + 1)

    def two(h):
        return pl.ds(al(h * 2 * W, 2 * W), 2 * W)

    def enc_copy(c):
        return to_chan(part.at[:, cols(c)], rs1.at[x], c_s.at[0, c], c_r.at[0, x], c)

    part[:, two(away)] = enc_sum[:, two(away)].astype(BF)
    for c in far:
        enc_copy(c).start()
    part[:, cols(twin)] = enc_sum[:, cols(twin)].astype(BF)
    enc_copy(twin).start()

    def late_copy(v, c):
        return to_chan(lat_out.at[v, rows_of(c), :], lat_in.at[x, v], l_s.at[v, c], l_r.at[v, x], c)

    for v in range(LATE // 2):
        t = T - LATE + 2 * v
        over_slots(t, t + 2, lambda t: grid_copy(t).wait_recv())
        lat_out[v] = embed(t // 2)[0]
        for c in (*far, twin):
            late_copy(v, c).start()
    load_mi.wait()

    def late_sum(c):
        out = jnp.zeros((MR, W), F32)
        for v in range(LATE // 2):
            here = pl.ds(al((c * LATE + 2 * v) * W, 2 * W), 2 * W)
            out = out + dot_nt(a_late[:, here], lat_in[c, v])
        return out

    lat_in[x] = lat_out[:, mine, :]
    enc_pre = enc_sum[:, mine] + late_sum(x)
    for dx in range(1, NX):
        p = peer(dx)
        to_chan(part.at[:, cols(p)], rs1.at[p], c_s.at[0, p], c_r.at[0, p], p).wait_recv()
        enc_pre = enc_pre + rs1[p].astype(F32)
    for c in (twin, *far):
        for v in range(LATE // 2):
            to_chan(lat_out.at[v, rows_of(c), :], lat_in.at[c, v], l_s.at[v, c], l_r.at[v, c], c).wait_recv()
        enc_pre = enc_pre + late_sum(c)
    enc_sig = jax.nn.sigmoid(enc_pre)
    mesh_one = (mi[...].astype(F32) + enc_pre * enc_sig).astype(BF)
    enc_slope = slope_of(enc_pre, enc_sig)
    enc_slope_f[...] = enc_slope

    ext[MR : 2 * MR, :] = mesh_one
    own_ext = ext.at[MR : 2 * MR, :]
    halo_up = to_band(own_ext, ext.at[0:MR, :], h_s.at[0], h_r.at[0], high)
    halo_down = to_band(own_ext, ext.at[2 * MR : 3 * MR, :], h_s.at[1], h_r.at[1], low)
    pl.when(has_high)(halo_up.start)
    pl.when(has_low)(halo_down.start)
    mid[...] = dot(a_proc[:, MR : 2 * MR], mesh_one)

    @pl.when(me == 0)
    def _():
        ext[0:MR, :] = jnp.zeros((MR, W), BF)

    @pl.when(me == NB - 1)
    def _():
        ext[2 * MR : 3 * MR, :] = jnp.zeros((MR, W), BF)

    pl.when(has_low)(halo_up.wait_recv)
    pl.when(has_high)(halo_down.wait_recv)
    proc_pre = (
        mid[...]
        + dot(a_proc[:, 0:MR], ext[0:MR, :])
        + dot(a_proc[:, 2 * MR : 3 * MR], ext[2 * MR : 3 * MR, :])
    )
    proc_sig = jax.nn.sigmoid(proc_pre)
    hidden = (proc_pre * proc_sig).astype(BF)
    hid_all[:, mine] = hidden

    def hid_copy(c):
        return to_chan(hid_all.at[:, mine], hid_all.at[:, mine], c_s.at[1, c], c_r.at[1, x], c)

    grad_proc = (gh[...] * slope_of(proc_pre, proc_sig)).astype(BF)

    hb_out[0] = dot(at_proc[0:MR, :], grad_proc).astype(BF)
    back_down = to_band(hb_out.at[0], hb_in.at[0], b_s.at[0], b_r.at[0], low)
    pl.when(has_low)(back_down.start)
    hb_out[1] = dot(at_proc[2 * MR : 3 * MR, :], grad_proc).astype(BF)
    back_up = to_band(hb_out.at[1], hb_in.at[1], b_s.at[1], b_r.at[1], high)
    pl.when(has_high)(back_up.start)
    mid[...] = dot(at_proc[MR : 2 * MR, :], grad_proc) + og_all[:, mine].astype(F32)

    gn_out[...] = dot(hidden.astype(F32).T.astype(BF), og_all[...])
    gn_in[mine, :] = gn_out[:, mine]

    def gn_copy(c):
        return to_chan(gn_out.at[:, cols(c)], gn_in.at[mine, :], c_s.at[2, c], c_r.at[2, x], c)

    for dx in range(1, NX):
        gn_copy(peer(dx)).start()

    @pl.when(me == NB - 1)
    def _():
        hb_in[0] = jnp.zeros((MR, W), BF)

    @pl.when(me == 0)
    def _():
        hb_in[1] = jnp.zeros((MR, W), BF)

    pl.when(has_high)(back_down.wait_recv)
    pl.when(has_low)(back_up.wait_recv)
    total = mid[...] + hb_in[0].astype(F32) + hb_in[1].astype(F32)
    mg[...] = total
    save_grad = pltpu.make_async_copy(mg, mesh_grad, lsem.at[1])
    save_grad.start()
    ge_all[mine, :] = (total * enc_slope_f[...]).T.astype(BF)

    def ge_copy(c):
        return to_chan(ge_all.at[mine, :], ge_all.at[mine, :], c_s.at[3, c], c_r.at[3, x], c)

    def ge_wait(c):
        to_chan(ge_all.at[rows_of(c), :], ge_all.at[rows_of(c), :], c_s.at[3, c], c_r.at[3, c], c).wait_recv()

    for c in (twin, *far):
        ge_copy(c).start()

    keep = pl.ds(al(core * 256, 256), 256)
    give = pl.ds(al((1 - core) * 256, 256), 256)
    pieces = (pieces_e, pieces_n)
    landed = (landed_e, landed_n)
    result = (fin_e, fin_n)
    other = (fin_e2, fin_n2)

    def z_of(j):
        return lax.rem(z_here + j, ZS)

    def sum_z(k, j):
        return to_band(pieces[k].at[z_of(j)], landed[k].at[z_here], u_s.at[k, j], u_r.at[k, j], at_z(j))

    def sum_y(k, j):
        return to_band(by_y.at[k, y_here], by_y.at[k, y_here], v_s.at[k, j], v_r.at[k, j], at_y(j))

    def back_z(k, j):
        return to_band(result[k].at[z_here], result[k].at[z_here], u_s.at[2 + k, j], u_r.at[2 + k, j], at_z(j))

    def start_z(k):
        for j in range(1, ZS):
            sum_z(k, j).start()
        landed[k][z_here] = pieces[k][z_here]

    def start_y(k):
        for j in range(1, ZS):
            sum_z(k, j).wait_recv()
        by_y[k, y_here] = jnp.sum(landed[k][...].astype(F32), axis=0)
        for j in range(1, YS):
            sum_y(k, j).start()

    def start_back(k):
        for j in range(1, YS):
            y = lax.rem(y_here - j + YS, YS)
            to_band(by_y.at[k, y], by_y.at[k, y], v_s.at[k, j], v_r.at[k, j], at_y(j)).wait_recv()
        result[k][z_here] = jnp.sum(by_y[k], axis=0).astype(result[k].dtype)
        for j in range(1, ZS):
            back_z(k, j).start()

    def swap_back(k):
        for j in range(1, ZS):
            z = lax.rem(z_here - j + ZS, ZS)
            to_band(result[k].at[z], result[k].at[z], u_s.at[2 + k, j], u_r.at[2 + k, j], at_z(j)).wait_recv()
        copy = to_band(result[k], other[k], t_s.at[2 + k], t_r.at[2 + k], sibling)
        copy.start()
        return copy

    for dx in range(1, NX):
        p = peer(dx)
        prow = pl.ds(al(p * W, W), W)
        to_chan(gn_out.at[:, cols(p)], gn_in.at[prow, :], c_s.at[2, p], c_r.at[2, p], p).wait_recv()
    node_swap = to_band(gn_in.at[give, :], node_in, t_s.at[0], t_r.at[0], sibling)
    node_swap.start()
    node_swap.wait_recv()
    pieces_n[...] = (gn_in[keep, :] + node_in[...]).reshape(ZS, ZR, W)
    start_z(1)

    gemb_f = enc_sum.at[0:CP, 0 : 2 * W]

    def back(h):
        def piece(t, _):
            here = pl.ds(al(t * 512, 512), 512)
            msg = dot(ge_all[two(h), :], a_enc[:, here])
            gp[:, here] = (msg * slope[two(h), here]).astype(BF)
            return 0

        lax.fori_loop(0, ER // 512, piece, 0)
        gemb_f[...] = dot_nt(recv[...], gp[...])

    keep_rows = pl.ds(al(core * HALF, 16), HALF)
    give_rows = pl.ds(al((1 - core) * HALF, 16), HALF)

    def half_copy(k):
        return to_band(half_out.at[k], half_in.at[k], h_s.at[2 + k], h_r.at[2 + k], sibling)

    def ge2_copy(c):
        return to_chan(gemb_out.at[:, cols(c)], rs2.at[x], c_s.at[4, c], c_r.at[4, x], c)

    ge_wait(twin)
    back(half)
    half_out[0] = gemb_f[give_rows, :]
    half_copy(0).start()
    half_f[0] = gemb_f[keep_rows, :]
    start_y(1)
    for c in far:
        ge_wait(c)
    back(away)
    half_out[1] = gemb_f[give_rows, :]
    half_copy(1).start()
    half_f[1] = gemb_f[keep_rows, :]
    half_copy(0).wait_recv()
    half_f[0] = half_f[0] + half_in[0]
    gemb_out[:, two(half)] = half_f[0].astype(BF)
    ge2_copy(twin).start()
    half_copy(1).wait_recv()
    gemb_out[:, two(away)] = (half_f[1] + half_in[1]).astype(BF)
    for c in far:
        ge2_copy(c).start()
    for dx in range(1, NX):
        hid_copy(peer(dx)).start()
    start_back(1)
    total = half_f[0, :, pl.ds(al(lax.rem(x, 2) * W, W), W)]
    for dx in range(1, NX):
        p = peer(dx)
        to_chan(gemb_out.at[:, cols(p)], rs2.at[p], c_s.at[4, p], c_r.at[4, p], p).wait_recv()
        total = total + rs2[p].astype(F32)
    padded = jnp.concatenate([total, jnp.zeros((ZS * ZR - HALF, W), F32)], axis=0)
    pieces_e[...] = padded.astype(BF).reshape(ZS, ZR, W)
    start_z(0)
    node_back = swap_back(1)
    start_y(0)
    start_back(0)

    for dx in range(1, NX):
        p = peer(dx)
        to_chan(hid_all.at[:, cols(p)], hid_all.at[:, cols(p)], c_s.at[1, p], c_r.at[1, p], p).wait_recv()
    mo[...] = (ext[MR : 2 * MR, :].astype(F32) + dot(hid_all[...], wn[...])).astype(BF)
    save_out = pltpu.make_async_copy(mo, mesh_out, lsem.at[2])
    save_out.start()
    node_back.wait_recv()
    node_saves = [pltpu.make_async_copy(fin_n, node_out, lsem.at[3]), pltpu.make_async_copy(fin_n2, node2_out, lsem.at[4])]
    for c in node_saves:
        c.start()
    last_back = swap_back(0)
    last_save = pltpu.make_async_copy(fin_e, fin_out, lsem.at[5])
    last_save.start()
    last_back.wait_recv()
    last_save2 = pltpu.make_async_copy(fin_e2, fin2_out, lsem.at[6])
    last_save2.start()
    saves = (*node_saves, last_save, last_save2)

    over_slots(T - LATE, T, lambda t: grid_copy(t).wait_send())
    for dx in range(1, NX):
        p = peer(dx)
        for c in early(dx):
            c.wait_send()
        for v in range(LATE // 2):
            late_copy(v, p).wait_send()
        for f in (enc_copy, hid_copy, gn_copy, ge_copy, ge2_copy):
            f(p).wait_send()
    pl.when(has_high)(halo_up.wait_send)
    pl.when(has_low)(halo_down.wait_send)
    pl.when(has_low)(back_down.wait_send)
    pl.when(has_high)(back_up.wait_send)
    for k in range(2):
        half_copy(k).wait_send()
    for c in (node_swap, node_back, last_back):
        c.wait_send()

    for k in range(2):
        for j in range(1, ZS):
            sum_z(k, j).wait_send()
            back_z(k, j).wait_send()
        for j in range(1, YS):
            sum_y(k, j).wait_send()
    save_grad.wait()
    save_out.wait()
    for c in saves:
        c.wait()


def on_device(
    grid_in, w_embed, send_order, enc_coef, enc_slot, enc_dest, mesh_in, proc_coef, proc_src, proc_dest, w_node, out_grad
):
    smem = pl.BlockSpec(memory_space=pltpu.SMEM)
    hbm = pl.BlockSpec(memory_space=pl.ANY)
    vmem = pl.BlockSpec(memory_space=pltpu.VMEM)
    V = pltpu.VMEM
    dma = pltpu.SemaphoreType.DMA
    piece = jax.ShapeDtypeStruct((ZS, ZR, W), F32)
    piece_bf = jax.ShapeDtypeStruct((ZS, ZR, W), BF)
    parts = pl.pallas_call(
        kernel,
        out_shape=(
            jax.ShapeDtypeStruct((MR, W), BF),
            jax.ShapeDtypeStruct((MR, W), F32),
            piece_bf, piece_bf, piece, piece,
        ),
        in_specs=[smem] + [vmem] * 4 + [hbm] * 7,
        out_specs=(hbm,) * 6,
        scratch_shapes=[
            V((2, W, NB * W), BF),
            V((C_IN - 3 * W, NB * W), BF),
            V((NB, W, W), BF),
            V((T, CP, W), BF),
            V((CP, ER), BF),
            V((LAT, CP), BF),
            V((C_IN, W), BF),
            V((MR, LAT), BF),
            V((LAT, W), BF),
            V((W, LAT), BF),
            V((MR, W), BF),
            V((EP * W, W), BF),
            V((EP * W, W), F32),
            V(((CELLS + LATE_CELLS) * W, W), F32),
            V((MR, ER), BF),
            V((MR, NX * LATE * W), BF),
            V((MR, 3 * MR), BF),
            V((3 * MR, MR), BF),
            V((MR, W), F32),
            V((LAT, ER), F32),
            V((MR, LAT), BF),
            V((MR, LAT), F32),
            V((MR, W), F32),
            V((NX, MR, W), BF),
            V((LATE // 2, LAT, 2 * W), BF),
            V((NX, LATE // 2, W, 2 * W), BF),
            V((3 * MR, W), BF),
            V((MR, LAT), BF),
            V((2, MR, W), BF),
            V((2, MR, W), BF),
            V((MR, W), F32),
            V((W, LAT), F32),
            V((LAT, W), F32),
            V((LAT, MR), BF),
            V((2 * W, ER), BF),
            V((2, HALF, 2 * W), F32),
            V((2, HALF, 2 * W), F32),
            V((2, HALF, 2 * W), F32),
            V((HALF, LAT), BF),
            V((NX, HALF, W), BF),
            V((256, W), F32),
            V((ZS, ZR, W), BF),
            V((ZS, ZR, W), F32),
            V((ZS, ZR, W), BF),
            V((ZS, ZR, W), F32),
            V((2, YS, ZR, W), F32),
            V((ZS, ZR, W), BF),
            V((ZS, ZR, W), BF),
            V((ZS, ZR, W), F32),
            V((ZS, ZR, W), F32),
            V((MR, W), BF),
            V((MR, W), F32),
            dma((7,)),
            dma((4,)),
            dma((FIRST,)), dma((FIRST,)),
            dma((T,)), dma((T,)),
            dma((3, NX)), dma((3, NX)),
            dma((4,)), dma((4,)),
            dma((2,)), dma((2,)),
            dma((5, NX)), dma((5, NX)),
            dma((4,)), dma((4,)),
            dma((4, ZS)), dma((4, ZS)),
            dma((2, YS)), dma((2, YS)),
            dma((LATE // 2, NX)), dma((LATE // 2, NX)),
        ],
        compiler_params=pltpu.CompilerParams(
            collective_id=0, has_side_effects=True, vmem_limit_bytes=60 << 20
        ),
    )(
        send_order, enc_slot, enc_dest, proc_src, proc_dest, grid_in.T,
        w_embed, enc_coef.reshape(EP * W, W), mesh_in,
        proc_coef.reshape(PP * W, W), w_node, out_grad,
    )
    return pl.pallas_call(
        finish,
        out_shape=(
            jax.ShapeDtypeStruct((MR, W), BF),
            jax.ShapeDtypeStruct((MR, W), F32),
            jax.ShapeDtypeStruct((C_IN, W), F32),
            jax.ShapeDtypeStruct((LAT, W), F32),
        ),
        in_specs=[vmem] * 6,
        out_specs=(vmem,) * 4,
        compiler_params=pltpu.CompilerParams(vmem_limit_bytes=60 << 20),
    )(*parts)


def solution(mesh):
    return jax.shard_map(
        on_device,
        mesh=mesh,
        in_specs=(
            P("band", None),
            P(None, "chan"),
            P("band", None),
            P("band", None, None),
            P("band", None),
            P("band", None),
            P("band", "chan"),
            P("band", None, None),
            P("band", None),
            P("band", None),
            P(None, "chan"),
            P("band", "chan"),
        ),
        out_specs=(P("band", "chan"), P("band", "chan"), P(None, "chan"), P(None, "chan")),
        check_vma=False,
    )
```

time: 131 us -> 127 us (0.969); the launches traced: 131 us -> 125 us
  local copies, waits for them, and re-layouts: 6.63 us -> 0 us
    unnamed x4 -> x0, local copies, waits for them, and re-layouts: 6.63 us -> none
    pallas_call x0 -> x1, Pallas kernels: none -> 2.19 us  [on_device(): pl.pallas_call(finish, out_shape=(jax.ShapeDtypeStruct((MR, W), BF), jax....]
    pallas_call x1, Pallas kernels: 124 us -> 122 us  [on_device(): pl.pallas_call(kernel, out_shape=(jax.ShapeDtypeStruct((MR, W), BF), jax....]
where the time goes in v2:
time: 127 us; the launch traced here: 125 us
  Pallas kernels  125 us (98%)
    pallas_call x1, Pallas kernels, on_device(): pl.pallas_call(kernel, out_shape=(jax.ShapeDtypeStruct((MR, W), BF), jax....  122 us

profile of v2, /device:TPU:1, one launch (start us, length us, event | category | flops | bytes accessed | tf_op | source)
XLA Modules:
  0.0 125.3 jit_solution(6632124141115921502)
XLA Ops:
  0.6 122.5 %shard_map.147 = (bf16[640,128]{1,0:T(8,128)(2,1)}, f32[640,128]{1,0:T(8,128)}, bf16[8,32,128]{2,1,0:T(8,128)(2,1)}, bf16[8,32,128]{2,1,0:T(8,128)(2,1)}, f32[8,32,128]{2,1,0:T(8,128)}, /*index=5*/f32[8,32,128]{2,1,0:T(8,128)}) custom-call(s32[1,64]{1,0:T(1,128)} %order.1, s32[1,96]{1,0:T(1,128)} %eslot.1, s32[1,96]{1,0:T(1,128)} %edest.1, s32[1,48]{1,0:T(1,128)} %psrc.1, ...), custom_call_target="tpu_custom_call" | custom-call | tf_op jit(solution)/shard_map/pallas_call | solution.py:615
  123.1 2.2 %shard_map.148 = (bf16[640,128]{1,0:T(8,128)(2,1)}, f32[640,128]{1,0:T(8,128)}, f32[474,128]{1,0:T(8,128)}, f32[512,128]{1,0:T(8,128)}) custom-call(bf16[640,128]{1,0:T(8,128)(2,1)} %get-tuple-element.10.out_in, f32[640,128]{1,0:T(8,128)} %get-tuple-element.11.grad_in, bf16[8,32,128]{2,1,0:T(8,128)(2,1)} %get-tuple-element.12.fin, ...), custom_call_target="tpu_custom_call" | custom-call | tf_op jit(solution)/shard_map/pallas_call | solution.py:698

commit v3 on v2

--- a/solution.py
+++ b/solution.py
@@ -21,13 +21,18 @@
 MR = MB * W
 ER = T * W
 CELLS = MB * T
-LATE = 4
+LATE = 2
 LATE_CELLS = MB * NX * LATE
+OWN = 1
 FIRST = 4
 ZS = 8
 YS = 4
 ZR = 32
 HALF = CP // 2
+
+
+def place_of(t):
+    return (3 * t + 13) & (T - 1)
 
 
 def dot(a, b):
@@ -151,7 +156,7 @@
 
     stage[:, CP - 16 :, :] = jnp.zeros((T, 16, W), BF)
     def band_of(t):
-        return lax.rem(me + x + NX * t, NB)
+        return lax.rem(me + x + NX * place_of(t), NB)
 
     def first_copy(t):
         rows = pl.ds(0, W)
@@ -166,7 +171,7 @@
 
     def over_slots(lo, hi, body):
         def one(t, _):
-            pl.when(x + t != 0)(lambda: body(t))
+            pl.when(x + place_of(t) != 0)(lambda: body(t))
             return 0
 
         lax.fori_loop(lo, hi, one, 0)
@@ -197,7 +202,7 @@
 
     @pl.when(x == 0)
     def _():
-        recv[:, 0:W] = stage[0]
+        recv[:, OWN * W : (OWN + 1) * W] = stage[OWN]
 
     load_wemb.wait()
     we_all[mine, CP - W : CP] = jnp.zeros((W, W), BF)
@@ -237,10 +242,10 @@
     cell = lax.broadcasted_iota(jnp.int32, (CELLS + LATE_CELLS, EP), 0)
     tail = cell - CELLS
     own_group = cell < CELLS
-    cell_m = jnp.where(own_group, lax.shift_right_logical(cell, 4), lax.shift_right_arithmetic(tail, 4))
+    cell_m = jnp.where(own_group, lax.shift_right_logical(cell, 4), lax.shift_right_arithmetic(tail, 3))
     cell_t = jnp.where(own_group, lax.bitwise_and(cell, T - 1), T - LATE + lax.bitwise_and(tail, LATE - 1))
-    cell_x = jnp.where(own_group, x, lax.bitwise_and(lax.shift_right_arithmetic(tail, 2), NX - 1))
-    cell_slot = lax.bitwise_and(me - cell_x - NX * cell_t + 2 * NB, NB - 1)
+    cell_x = jnp.where(own_group, x, lax.bitwise_and(lax.shift_right_arithmetic(tail, 1), NX - 1))
+    cell_slot = lax.bitwise_and(me - cell_x - NX * place_of(cell_t) + 2 * NB, NB - 1)
     sum_cells(ce, EP, CELLS + LATE_CELLS, (edest[...] == cell_m) & (eslot[...] == cell_slot))
 
     load_cp.start()
@@ -539,8 +544,6 @@
     gemb_out[:, two(away)] = (half_f[1] + half_in[1]).astype(BF)
     for c in far:
         ge2_copy(c).start()
-    for dx in range(1, NX):
-        hid_copy(peer(dx)).start()
     start_back(1)
     total = half_f[0, :, pl.ds(al(lax.rem(x, 2) * W, W), W)]
     for dx in range(1, NX):
@@ -550,6 +553,8 @@
     padded = jnp.concatenate([total, jnp.zeros((ZS * ZR - HALF, W), F32)], axis=0)
     pieces_e[...] = padded.astype(BF).reshape(ZS, ZR, W)
     start_z(0)
+    for dx in range(1, NX):
+        hid_copy(peer(dx)).start()
     node_back = swap_back(1)
     start_y(0)
     start_back(0)

time: 127 us -> 117 us (0.921); the launches traced: 125 us -> 117 us
  Pallas kernels: 125 us -> 116 us
    pallas_call x1, Pallas kernels: 122 us -> 114 us  [on_device(): pl.pallas_call(kernel, out_shape=(jax.ShapeDtypeStruct((MR, W), BF), jax....]
where the time goes in v3:
time: 117 us
  Pallas kernels  116 us (99%)
    pallas_call x1, Pallas kernels, on_device(): pl.pallas_call(kernel, out_shape=(jax.ShapeDtypeStruct((MR, W), BF), jax....  114 us

profile of v3, /device:TPU:1, one launch (start us, length us, event | category | flops | bytes accessed | tf_op | source)
XLA Modules:
  0.0 116.9 jit_solution(18020950959642639582)
XLA Ops:
  0.6 114.0 %shard_map.147 = (bf16[640,128]{1,0:T(8,128)(2,1)}, f32[640,128]{1,0:T(8,128)}, bf16[8,32,128]{2,1,0:T(8,128)(2,1)}, bf16[8,32,128]{2,1,0:T(8,128)(2,1)}, f32[8,32,128]{2,1,0:T(8,128)}, /*index=5*/f32[8,32,128]{2,1,0:T(8,128)}) custom-call(s32[1,64]{1,0:T(1,128)} %order.1, s32[1,96]{1,0:T(1,128)} %eslot.1, s32[1,96]{1,0:T(1,128)} %edest.1, s32[1,48]{1,0:T(1,128)} %psrc.1, ...), custom_call_target="tpu_custom_call" | custom-call | tf_op jit(solution)/shard_map/pallas_call | solution.py:620
  114.7 2.2 %shard_map.148 = (bf16[640,128]{1,0:T(8,128)(2,1)}, f32[640,128]{1,0:T(8,128)}, f32[474,128]{1,0:T(8,128)}, f32[512,128]{1,0:T(8,128)}) custom-call(bf16[640,128]{1,0:T(8,128)(2,1)} %get-tuple-element.10.out_in, f32[640,128]{1,0:T(8,128)} %get-tuple-element.11.grad_in, bf16[8,32,128]{2,1,0:T(8,128)(2,1)} %get-tuple-element.12.fin, ...), custom_call_target="tpu_custom_call" | custom-call | tf_op jit(solution)/shard_map/pallas_call | solution.py:703

commit v4 on v3

--- a/solution.py
+++ b/solution.py
@@ -97,6 +97,45 @@
     def rows_of(c):
         return pl.ds(al(c * W, W), W)
 
+    barrier = pltpu.get_barrier_semaphore()
+
+    def greet(band):
+        pl.semaphore_signal(barrier, inc=1, device_id={"band": band}, device_id_type=MESH)
+
+    z_here = lax.div(me, 8)
+    y_here = lax.rem(chip, YS)
+    has_low = me > 0
+    has_high = me < NB - 1
+    low = lax.rem(me + NB - 1, NB)
+    high = lax.rem(me + 1, NB)
+    sibling = me + 1 - 2 * core
+
+    def at_z(j):
+        return lax.rem(me + 8 * j, NB)
+
+    def at_y(j):
+        return z_here * 8 + lax.rem(y_here + j, YS) * 2 + core
+
+    def greet_source(t, _):
+        @pl.when(x + t != 0)
+        def _():
+            greet(lax.rem(me - x - NX * t + 2 * NB, NB))
+
+        return 0
+
+    lax.fori_loop(0, T, greet_source, 0)
+    pl.when(has_low)(lambda: greet(low))
+    pl.when(has_high)(lambda: greet(high))
+    greet(sibling)
+    for j in range(1, ZS):
+        greet(at_z(j))
+    for j in range(1, YS):
+        greet(at_y(j))
+    for dx in range(1, NX):
+        pl.semaphore_signal(barrier, inc=1, device_id={"chan": peer(dx)}, device_id_type=MESH)
+    greetings = T + 2 + 1 + ZS - 1 + YS - 1 + NX - 1
+    absent = jnp.where(x == 0, 1, 0) + jnp.where(me == 0, 1, 0) + jnp.where(me == NB - 1, 1, 0)
+
     steps = ((0, 128), (128, 256), (256, 384), (384, C_IN))
     load_grid = [
         pltpu.make_async_copy(grid.at[a:b, :], flat_last if i == 3 else flat.at[i % 2], g_s.at[i])
@@ -115,45 +154,6 @@
     load_og.start()
     load_wn.start()
 
-    barrier = pltpu.get_barrier_semaphore()
-
-    def greet(band):
-        pl.semaphore_signal(barrier, inc=1, device_id={"band": band}, device_id_type=MESH)
-
-    z_here = lax.div(me, 8)
-    y_here = lax.rem(chip, YS)
-    has_low = me > 0
-    has_high = me < NB - 1
-    low = lax.rem(me + NB - 1, NB)
-    high = lax.rem(me + 1, NB)
-    sibling = me + 1 - 2 * core
-
-    def at_z(j):
-        return lax.rem(me + 8 * j, NB)
-
-    def at_y(j):
-        return z_here * 8 + lax.rem(y_here + j, YS) * 2 + core
-
-    def greet_source(t, _):
-        @pl.when(x + t != 0)
-        def _():
-            greet(lax.rem(me - x - NX * t + 2 * NB, NB))
-
-        return 0
-
-    lax.fori_loop(0, T, greet_source, 0)
-    pl.when(has_low)(lambda: greet(low))
-    pl.when(has_high)(lambda: greet(high))
-    greet(sibling)
-    for j in range(1, ZS):
-        greet(at_z(j))
-    for j in range(1, YS):
-        greet(at_y(j))
-    for dx in range(1, NX):
-        pl.semaphore_signal(barrier, inc=1, device_id={"chan": peer(dx)}, device_id_type=MESH)
-    greetings = T + 2 + 1 + ZS - 1 + YS - 1 + NX - 1
-    absent = jnp.where(x == 0, 1, 0) + jnp.where(me == 0, 1, 0) + jnp.where(me == NB - 1, 1, 0)
-
     stage[:, CP - 16 :, :] = jnp.zeros((T, 16, W), BF)
     def band_of(t):
         return lax.rem(me + x + NX * place_of(t), NB)
@@ -287,23 +287,24 @@
         rest_copy(t).wait_send()
 
     over_slots(0, FIRST, sent_first)
-    over_slots(FIRST, T - LATE, lambda t: grid_copy(t).wait_send())
+    over_slots(FIRST, 8, lambda t: grid_copy(t).wait_send())
     over_slots(T - LATE, T, lambda t: grid_copy(t).start())
+    over_slots(8, T - LATE, lambda t: grid_copy(t).wait_send())
 
     def dot_nt(a, b):
         return lax.dot_general(a, b, (((1,), (1,)), ((), ())), preferred_element_type=F32)
 
     enc_sum[...] = jnp.zeros((MR, LAT), F32)
 
-    def embed(u):
-        here = pl.ds(al(u * 2 * W, 2 * W), 2 * W)
+    def embed(here):
         pre = dot(we_all[...], recv[:, here])
         sig = jax.nn.sigmoid(pre)
         slope[:, here] = slope_of(pre, sig)
-        return (pre * sig).astype(BF), here
+        return (pre * sig).astype(BF)
 
     def embed_sum(u, _):
-        latent, here = embed(u)
+        here = pl.ds(al(u * 2 * W, 2 * W), 2 * W)
+        latent = embed(here)
         enc_sum[...] += dot_nt(a_enc[:, here], latent)
         return 0
 
@@ -342,19 +343,18 @@
     def late_copy(v, c):
         return to_chan(lat_out.at[v, rows_of(c), :], lat_in.at[x, v], l_s.at[v, c], l_r.at[v, x], c)
 
-    for v in range(LATE // 2):
-        t = T - LATE + 2 * v
-        over_slots(t, t + 2, lambda t: grid_copy(t).wait_recv())
-        lat_out[v] = embed(t // 2)[0]
+    for v in range(LATE):
+        t = T - LATE + v
+        grid_copy(t).wait_recv()
+        lat_out[v] = embed(pl.ds(t * W, W))
         for c in (*far, twin):
             late_copy(v, c).start()
     load_mi.wait()
 
     def late_sum(c):
         out = jnp.zeros((MR, W), F32)
-        for v in range(LATE // 2):
-            here = pl.ds(al((c * LATE + 2 * v) * W, 2 * W), 2 * W)
-            out = out + dot_nt(a_late[:, here], lat_in[c, v])
+        for v in range(LATE):
+            out = out + dot_nt(a_late[:, cols(c * LATE + v)], lat_in[c, v])
         return out
 
     lat_in[x] = lat_out[:, mine, :]
@@ -364,7 +364,7 @@
         to_chan(part.at[:, cols(p)], rs1.at[p], c_s.at[0, p], c_r.at[0, p], p).wait_recv()
         enc_pre = enc_pre + rs1[p].astype(F32)
     for c in (twin, *far):
-        for v in range(LATE // 2):
+        for v in range(LATE):
             to_chan(lat_out.at[v, rows_of(c), :], lat_in.at[c, v], l_s.at[v, c], l_r.at[v, c], c).wait_recv()
         enc_pre = enc_pre + late_sum(c)
     enc_sig = jax.nn.sigmoid(enc_pre)
@@ -389,12 +389,9 @@
         ext[2 * MR : 3 * MR, :] = jnp.zeros((MR, W), BF)
 
     pl.when(has_low)(halo_up.wait_recv)
+    mid[...] += dot(a_proc[:, 0:MR], ext[0:MR, :])
     pl.when(has_high)(halo_down.wait_recv)
-    proc_pre = (
-        mid[...]
-        + dot(a_proc[:, 0:MR], ext[0:MR, :])
-        + dot(a_proc[:, 2 * MR : 3 * MR], ext[2 * MR : 3 * MR, :])
-    )
+    proc_pre = mid[...] + dot(a_proc[:, 2 * MR : 3 * MR], ext[2 * MR : 3 * MR, :])
     proc_sig = jax.nn.sigmoid(proc_pre)
     hidden = (proc_pre * proc_sig).astype(BF)
     hid_all[:, mine] = hidden
@@ -582,7 +579,7 @@
         p = peer(dx)
         for c in early(dx):
             c.wait_send()
-        for v in range(LATE // 2):
+        for v in range(LATE):
             late_copy(v, p).wait_send()
         for f in (enc_copy, hid_copy, gn_copy, ge_copy, ge2_copy):
             f(p).wait_send()
@@ -651,8 +648,8 @@
             V((MR, LAT), F32),
             V((MR, W), F32),
             V((NX, MR, W), BF),
-            V((LATE // 2, LAT, 2 * W), BF),
-            V((NX, LATE // 2, W, 2 * W), BF),
+            V((LATE, LAT, W), BF),
+            V((NX, LATE, W, W), BF),
             V((3 * MR, W), BF),
             V((MR, LAT), BF),
             V((2, MR, W), BF),
@@ -690,7 +687,7 @@
             dma((4,)), dma((4,)),
             dma((4, ZS)), dma((4, ZS)),
             dma((2, YS)), dma((2, YS)),
-            dma((LATE // 2, NX)), dma((LATE // 2, NX)),
+            dma((LATE, NX)), dma((LATE, NX)),
         ],
         compiler_params=pltpu.CompilerParams(
             collective_id=0, has_side_effects=True, vmem_limit_bytes=60 << 20

time: 117 us -> 115 us (0.983)
  Pallas kernels: 116 us -> 114 us
    pallas_call x1, Pallas kernels: 114 us -> 112 us  [on_device(): pl.pallas_call(kernel, out_shape=(jax.ShapeDtypeStruct((MR, W), BF), jax....]
where the time goes in v4:
time: 115 us
  Pallas kernels  114 us (99%)
    pallas_call x1, Pallas kernels, on_device(): pl.pallas_call(kernel, out_shape=(jax.ShapeDtypeStruct((MR, W), BF), jax....  112 us

profile of v4, /device:TPU:1, one launch (start us, length us, event | category | flops | bytes accessed | tf_op | source)
XLA Modules:
  0.0 115.1 jit_solution(3240771656527405358)
XLA Ops:
  0.6 112.2 %shard_map.147 = (bf16[640,128]{1,0:T(8,128)(2,1)}, f32[640,128]{1,0:T(8,128)}, bf16[8,32,128]{2,1,0:T(8,128)(2,1)}, bf16[8,32,128]{2,1,0:T(8,128)(2,1)}, f32[8,32,128]{2,1,0:T(8,128)}, /*index=5*/f32[8,32,128]{2,1,0:T(8,128)}) custom-call(s32[1,64]{1,0:T(1,128)} %order.1, s32[1,96]{1,0:T(1,128)} %eslot.1, s32[1,96]{1,0:T(1,128)} %edest.1, s32[1,48]{1,0:T(1,128)} %psrc.1, ...), custom_call_target="tpu_custom_call" | custom-call | tf_op jit(solution)/shard_map/pallas_call | solution.py:617
  112.9 2.2 %shard_map.148 = (bf16[640,128]{1,0:T(8,128)(2,1)}, f32[640,128]{1,0:T(8,128)}, f32[474,128]{1,0:T(8,128)}, f32[512,128]{1,0:T(8,128)}) custom-call(bf16[640,128]{1,0:T(8,128)(2,1)} %get-tuple-element.10.out_in, f32[640,128]{1,0:T(8,128)} %get-tuple-element.11.grad_in, bf16[8,32,128]{2,1,0:T(8,128)(2,1)} %get-tuple-element.12.fin, ...), custom_call_target="tpu_custom_call" | custom-call | tf_op jit(solution)/shard_map/pallas_call | solution.py:700

commit v5 on v4

--- a/solution.py
+++ b/solution.py
@@ -68,13 +68,13 @@
 
 
 def kernel(
-    order, eslot, edest, psrc, pdest, grid, wemb, ecoef, meshin, pcoef, wnode, ograd,
+    order_in, eslot_in, edest_in, psrc_in, pdest_in, grid, wemb, ecoef, meshin, pcoef, wnode, ograd,
     mesh_out, mesh_grad, fin_out, fin2_out, node_out, node2_out,
-    flat, flat_last, blocks, stage, recv, we_all, wtmp, og_all, wn, wr_all, mi, ce,
+    order, eslot, edest, psrc, pdest, flat, flat_last, blocks, stage, recv, we_all, wtmp, og_all, wn, wr_all, mi, ce,
     wide, cells, a_enc, a_late, a_proc, at_proc, gh, slope,
     part, enc_sum, enc_slope_f, rs1, lat_out, lat_in, ext, hid_all, hb_out, hb_in, mid, gn_out, gn_in, ge_all, gp,
     half_f, half_out, half_in, gemb_out, rs2, node_in, pieces_e, pieces_n, landed_e, landed_n, by_y, fin_e, fin_e2, fin_n, fin_n2, mo, mg,
-    lsem, g_s, f_s, f_r, a_s, a_r, x_s, x_r, h_s, h_r, b_s, b_r, c_s, c_r, t_s, t_r, u_s, u_r, v_s, v_r, l_s, l_r,
+    lsem, i_s, g_s, f_s, f_r, a_s, a_r, x_s, x_r, h_s, h_r, b_s, b_r, c_s, c_r, t_s, t_r, u_s, u_r, v_s, v_r, l_s, l_r,
 ):
     me = lax.axis_index("band")
     x = lax.axis_index("chan")
@@ -136,6 +136,9 @@
     greetings = T + 2 + 1 + ZS - 1 + YS - 1 + NX - 1
     absent = jnp.where(x == 0, 1, 0) + jnp.where(me == 0, 1, 0) + jnp.where(me == NB - 1, 1, 0)
 
+    ids = ((order_in, order), (eslot_in, eslot), (edest_in, edest), (psrc_in, psrc), (pdest_in, pdest))
+    load_ids = [pltpu.make_async_copy(src, dst, i_s.at[i]) for i, (src, dst) in enumerate(ids)]
+    load_ids[0].start()
     steps = ((0, 128), (128, 256), (256, 384), (384, C_IN))
     load_grid = [
         pltpu.make_async_copy(grid.at[a:b, :], flat_last if i == 3 else flat.at[i % 2], g_s.at[i])
@@ -150,6 +153,8 @@
     load_ce = pltpu.make_async_copy(ecoef, ce, lsem.at[5])
     cp = ce.at[0 : PP * W, :]
     load_cp = pltpu.make_async_copy(pcoef, cp, lsem.at[6])
+    for c in load_ids[1:]:
+        c.start()
     load_wemb.start()
     load_og.start()
     load_wn.start()
@@ -186,6 +191,9 @@
         lax.fori_loop(0, NB, by_block, 0, unroll=4)
         if i == 0:
             load_grid[2].start()
+
+        if i == 0:
+            load_ids[0].wait()
 
         def to_stage(t, _, a=a, b=b):
             stage[t, a:b, :] = blocks[order[0, band_of(t)], 0 : b - a, :]
@@ -238,6 +246,8 @@
         cell = lax.broadcasted_iota(jnp.int32, (CELLS, pairs), 0)
         return lax.shift_right_logical(cell, 4), lax.bitwise_and(cell, T - 1)
 
+    for c in load_ids[1:]:
+        c.wait()
     load_ce.wait()
     cell = lax.broadcasted_iota(jnp.int32, (CELLS + LATE_CELLS, EP), 0)
     tail = cell - CELLS
@@ -607,7 +617,6 @@
 def on_device(
     grid_in, w_embed, send_order, enc_coef, enc_slot, enc_dest, mesh_in, proc_coef, proc_src, proc_dest, w_node, out_grad
 ):
-    smem = pl.BlockSpec(memory_space=pltpu.SMEM)
     hbm = pl.BlockSpec(memory_space=pl.ANY)
     vmem = pl.BlockSpec(memory_space=pltpu.VMEM)
     V = pltpu.VMEM
@@ -621,9 +630,14 @@
             jax.ShapeDtypeStruct((MR, W), F32),
             piece_bf, piece_bf, piece, piece,
         ),
-        in_specs=[smem] + [vmem] * 4 + [hbm] * 7,
+        in_specs=[hbm] * 12,
         out_specs=(hbm,) * 6,
         scratch_shapes=[
+            pltpu.SMEM((1, NB), jnp.int32),
+            V((1, EP), jnp.int32),
+            V((1, EP), jnp.int32),
+            V((1, PP), jnp.int32),
+            V((1, PP), jnp.int32),
             V((2, W, NB * W), BF),
             V((C_IN - 3 * W, NB * W), BF),
             V((NB, W, W), BF),
@@ -677,6 +691,7 @@
             V((MR, W), BF),
             V((MR, W), F32),
             dma((7,)),
+            dma((5,)),
             dma((4,)),
             dma((FIRST,)), dma((FIRST,)),
             dma((T,)), dma((T,)),

time: 115 us -> 114 us (level)
  no operation moved by 1% of the time
where the time goes in v5:
time: 114 us
  Pallas kernels  114 us (100%)
    pallas_call x1, Pallas kernels, on_device(): pl.pallas_call(kernel, out_shape=(jax.ShapeDtypeStruct((MR, W), BF), jax....  111 us

profile of v5, /device:TPU:1, one launch (start us, length us, event | category | flops | bytes accessed | tf_op | source)
XLA Modules:
  0.0 114.2 jit_solution(2693215518269126832)
XLA Ops:
  0.6 111.4 %shard_map.147 = (bf16[640,128]{1,0:T(8,128)(2,1)}, f32[640,128]{1,0:T(8,128)}, bf16[8,32,128]{2,1,0:T(8,128)(2,1)}, bf16[8,32,128]{2,1,0:T(8,128)(2,1)}, f32[8,32,128]{2,1,0:T(8,128)}, /*index=5*/f32[8,32,128]{2,1,0:T(8,128)}) custom-call(s32[1,64]{1,0:T(1,128)} %order_in.1, s32[1,96]{1,0:T(1,128)} %eslot_in.1, s32[1,96]{1,0:T(1,128)} %edest_in.1, ...), custom_call_target="tpu_custom_call" | custom-call | tf_op jit(solution)/shard_map/pallas_call | solution.py:626
  112.0 2.2 %shard_map.148 = (bf16[640,128]{1,0:T(8,128)(2,1)}, f32[640,128]{1,0:T(8,128)}, f32[474,128]{1,0:T(8,128)}, f32[512,128]{1,0:T(8,128)}) custom-call(bf16[640,128]{1,0:T(8,128)(2,1)} %get-tuple-element.10.out_in, f32[640,128]{1,0:T(8,128)} %get-tuple-element.11.grad_in, bf16[8,32,128]{2,1,0:T(8,128)(2,1)} %get-tuple-element.12.fin, ...), custom_call_target="tpu_custom_call" | custom-call | tf_op jit(solution)/shard_map/pallas_call | solution.py:715

commit v6 on v5

--- a/solution.py
+++ b/solution.py
@@ -97,6 +97,13 @@
     def rows_of(c):
         return pl.ds(al(c * W, W), W)
 
+    steps = ((0, 128), (128, 256), (256, 384), (384, C_IN))
+    load_grid = [
+        pltpu.make_async_copy(grid.at[a:b, :], flat_last if i == 3 else flat.at[i % 2], g_s.at[i])
+        for i, (a, b) in enumerate(steps)
+    ]
+    load_grid[0].start()
+
     barrier = pltpu.get_barrier_semaphore()
 
     def greet(band):
@@ -139,12 +146,7 @@
     ids = ((order_in, order), (eslot_in, eslot), (edest_in, edest), (psrc_in, psrc), (pdest_in, pdest))
     load_ids = [pltpu.make_async_copy(src, dst, i_s.at[i]) for i, (src, dst) in enumerate(ids)]
     load_ids[0].start()
-    steps = ((0, 128), (128, 256), (256, 384), (384, C_IN))
-    load_grid = [
-        pltpu.make_async_copy(grid.at[a:b, :], flat_last if i == 3 else flat.at[i % 2], g_s.at[i])
-        for i, (a, b) in enumerate(steps)
-    ]
-    for i in (0, 1, 3):
+    for i in (1, 3):
         load_grid[i].start()
     load_wemb = pltpu.make_async_copy(wemb, wtmp, lsem.at[1])
     load_og = pltpu.make_async_copy(ograd, og_all.at[:, mine], lsem.at[2])

time: 114 us -> 115 us (level)
  no operation moved by 1% of the time
where the time goes in v6:
time: 115 us
  Pallas kernels  114 us (99%)
    pallas_call x1, Pallas kernels, on_device(): pl.pallas_call(kernel, out_shape=(jax.ShapeDtypeStruct((MR, W), BF), jax....  112 us

profile of v6, /device:TPU:1, one launch (start us, length us, event | category | flops | bytes accessed | tf_op | source)
XLA Modules:
  0.0 115.1 jit_solution(7036172248820164756)
XLA Ops:
  0.6 112.2 %shard_map.147 = (bf16[640,128]{1,0:T(8,128)(2,1)}, f32[640,128]{1,0:T(8,128)}, bf16[8,32,128]{2,1,0:T(8,128)(2,1)}, bf16[8,32,128]{2,1,0:T(8,128)(2,1)}, f32[8,32,128]{2,1,0:T(8,128)}, /*index=5*/f32[8,32,128]{2,1,0:T(8,128)}) custom-call(s32[1,64]{1,0:T(1,128)} %order_in.1, s32[1,96]{1,0:T(1,128)} %eslot_in.1, s32[1,96]{1,0:T(1,128)} %edest_in.1, ...), custom_call_target="tpu_custom_call" | custom-call | tf_op jit(solution)/shard_map/pallas_call | solution.py:628
  112.9 2.2 %shard_map.148 = (bf16[640,128]{1,0:T(8,128)(2,1)}, f32[640,128]{1,0:T(8,128)}, f32[474,128]{1,0:T(8,128)}, f32[512,128]{1,0:T(8,128)}) custom-call(bf16[640,128]{1,0:T(8,128)(2,1)} %get-tuple-element.10.out_in, f32[640,128]{1,0:T(8,128)} %get-tuple-element.11.grad_in, bf16[8,32,128]{2,1,0:T(8,128)(2,1)} %get-tuple-element.12.fin, ...), custom_call_target="tpu_custom_call" | custom-call | tf_op jit(solution)/shard_map/pallas_call | solution.py:717
